TPU v7x, 256 devices: a whole 4x4x8 slice. The times are simulated.
256 devices in a mesh: space: 64 (over z, x, core), dir: 4 (over y).
Axes of the slice: x: 4, y: 4, z: 8, core: 2. Of those that a mesh axis runs over, the one named last changes fastest.
Arguments:
- directions: bfloat16 [128, 512, 2048], P('dir', 'space'), may hold values from -16 to 16
- depth_coef: float32 [512, 2048], P('space'), may hold values from 0.5 to 2
- sensitivity: float32 [512, 2048], P('space'), may hold values from 0.4 to 1.6
- obs_weight: float32 [512, 2048], P('space'), may hold values from 0.4 to 1.6
Outputs:
- basis: bfloat16 [128, 512, 2048], P('dir', 'space')
- factor: float32 [128, 128], replicated
All inputs are finite; a program needn't handle non-finite values.
Results may differ from a plain program's by a relative error of at most 0.001.
Values may be sent and summed in bfloat16 or wider, within the bound.
A program may use at most 64 MiB of HBM per device.

v0:
```python
import jax
import jax.numpy as jnp
from jax import lax
from jax.sharding import PartitionSpec as P


def with_halo(block, sides, width):
    for axis, dim in sides:
        count = lax.axis_size(axis)
        forward = [(i, i + 1) for i in range(count - 1)]
        backward = [(target, source) for source, target in forward]
        low = lax.ppermute(
            lax.slice_in_dim(block, block.shape[dim] - width, None, axis=dim), axis, forward
        )
        high = lax.ppermute(lax.slice_in_dim(block, 0, width, axis=dim), axis, backward)
        block = jnp.concatenate([low, block, high], axis=dim)
    return block


def laplace(extended):
    inner = extended[..., 1:-1, 1:-1]
    return (
        extended[..., :-2, 1:-1]
        + extended[..., 2:, 1:-1]
        + extended[..., 1:-1, :-2]
        + extended[..., 1:-1, 2:]
        - 4.0 * inner
    )


def sideways(extended, width):
    return jnp.pad(extended, ((0, 0), (0, 0), (width, width)))


def neighbours(field):
    return laplace(sideways(with_halo(field, (("space", 1),), 1), 1))


def invert_lower(lower_factor):
    width = lower_factor.shape[0]
    return lax.linalg.triangular_solve(
        lower_factor, jnp.eye(width, dtype=jnp.float32), left_side=True, lower=True
    )


def per_device(directions, depth_coef, sensitivity, obs_weight):
    total_columns = depth_coef.shape[1]
    field = directions.astype(jnp.float32)
    prior = field + 0.1 * neighbours(field)
    state_one = sensitivity * prior
    state_two = state_one + 0.1 * depth_coef * neighbours(state_one) + sensitivity * prior
    misfit = obs_weight * state_two
    adjoint = misfit + 0.1 * neighbours(depth_coef * misfit)
    source = sensitivity * (misfit + adjoint)
    sketch = field + source + 0.1 * neighbours(source)
    local_dirs, rows_here, columns = sketch.shape
    cells = lax.axis_size("space") * rows_here * total_columns
    flat = sketch.reshape(local_dirs, rows_here * columns)
    regrouped = lax.all_to_all(flat, "dir", split_axis=1, concat_axis=0, tiled=True)
    partial_gram = (
        jnp.dot(
            regrouped,
            regrouped.T,
            precision=lax.Precision.HIGHEST,
            preferred_element_type=jnp.float32,
        )
        / cells
    )
    gram_total = lax.psum(partial_gram, ("space", "dir"))
    lower_factor = jnp.linalg.cholesky(gram_total)
    inverse = invert_lower(lower_factor)
    basis_rows = jnp.dot(
        inverse, regrouped, precision=lax.Precision.HIGHEST, preferred_element_type=jnp.float32
    )
    returned = lax.all_to_all(
        basis_rows.astype(jnp.bfloat16), "dir", split_axis=0, concat_axis=1, tiled=True
    )
    basis = returned.reshape(returned.shape[0], rows_here, columns)
    return (basis, lower_factor.T)


def solution(mesh):
    return jax.shard_map(
        per_device,
        mesh=mesh,
        in_specs=(P("dir", "space", None), P("space", None), P("space", None), P("space", None)),
        out_specs=(P("dir", "space", None), P()),
        check_vma=False,
    )
```

profile of v0, /device:TPU:1, one launch (start us, length us, event | category | flops | bytes accessed | tf_op | source)
XLA Modules:
  0.0 399.3 jit_solution(4084296628389579087)
XLA Ops:
  7.2 1.8 copy_convert_fusion
  9.1 4.5 %collective-permute-start = (f32[32,1,2048]{2,0,1:T(8,128)S(1)}, f32[32,1,2048]{2,0,1:T(8,128)S(1)}, u32[]{:S(2)}, u32[]{:S(2)}) collective-permute-start(f32[32,1,2048]{2,0,1:T(8,128)S(1)} %get-tuple-element.18), channel_id=1, source_target_pairs={{0,4},{4,8},{8,12},{12,16},{16,20},{20,24},{24,28},{28,32},{32,36}... | collective-permute-start | bytes 786440 | tf_op jit(solution)/shard_map/ppermute | solution.py:12
  13.6 2.1 collective-permute-start.1
  16.9 4.5 %collective-permute-done.1 = f32[32,1,2048]{2,0,1:T(8,128)S(1)} collective-permute-done((f32[32,1,2048]{2,0,1:T(8,128)S(1)}, f32[32,1,2048]{2,0,1:T(8,128)S(1)}, u32[]{:S(2)}, u32[]{:S(2)}) %collective-permute-start.1) | collective-permute-done | bytes 262176 | tf_op jit(solution)/shard_map/ppermute | solution.py:15
  23.3 1.9 collective-permute-start.2
  25.2 2.4 collective-permute-start.3
  28.5 4.4 %collective-permute-done.3 = f32[32,1,2048]{2,0,1:T(8,128)S(1)} collective-permute-done((f32[32,1,2048]{2,0,1:T(8,128)S(1)}, f32[32,1,2048]{2,0,1:T(8,128)S(1)}, u32[]{:S(2)}, u32[]{:S(2)}) %collective-permute-start.3) | collective-permute-done | bytes 262176 | tf_op jit(solution)/shard_map/ppermute | solution.py:15
  33.7 1.5 broadcast_multiply_fusion
  35.3 1.9 collective-permute-start.4
  37.2 2.4 collective-permute-start.5
  40.5 4.4 %collective-permute-done.5 = f32[32,1,2048]{2,0,1:T(8,128)S(1)} collective-permute-done((f32[32,1,2048]{2,0,1:T(8,128)S(1)}, f32[32,1,2048]{2,0,1:T(8,128)S(1)}, u32[]{:S(2)}, u32[]{:S(2)}) %collective-permute-start.5) | collective-permute-done | bytes 262176 | tf_op jit(solution)/shard_map/ppermute | solution.py:15
  46.7 1.9 collective-permute-start.6
  48.6 2.5 collective-permute-start.7
  51.9 6.3 %collective-permute-done.7 = f32[32,1,2048]{2,0,1:T(8,128)S(1)} collective-permute-done((f32[32,1,2048]{2,0,1:T(8,128)S(1)}, f32[32,1,2048]{2,0,1:T(8,128)S(1)}, u32[]{:S(2)}, u32[]{:S(2)}) %collective-permute-start.7) | collective-permute-done | bytes 262176 | tf_op jit(solution)/shard_map/ppermute | solution.py:15
  61.4 2.1 all_to_all.26
  63.5 2.8 copy.21
  66.3 25.8 %all_to_all.35 = f32[32,4,4096]{2,0,1:T(8,128)S(1)} all-to-all(f32[32,4,4096]{2,0,1:T(8,128)S(1)} %copy.21), channel_id=1, replica_groups=mesh['space'=64,'dir'=4] {'dir'}, dimensions={1} | all-to-all | bytes 4194304 | tf_op jit(solution)/shard_map/all_to_all | solution.py:59
  92.1 2.4 convolution_multiply_fusion
  94.6 249.7 %all-reduce.6.cloned.1.call-done = f32[128,128]{0,1:T(8,128)} async-done(((f32[128,128]{0,1:T(8,128)}), f32[128,128]{0,1:T(8,128)}) %all-reduce.6.cloned.1.call-update) | async-done | bytes 65552 | tf_op jit(solution)/shard_map/psum | solution.py:69
  346.1 11.7 %cholesky.17 = f32[128,128]{1,0:T(8,128)S(1)} custom-call(f32[128,128]{1,0:T(8,128)S(1)} %fusion.20), custom_call_target="Cholesky" | custom-call | tf_op jit(solution)/shard_map/jit(cholesky)/cholesky | solution.py:70
  359.1 9.8 %custom-call.6 = f32[1,128,128]{1,2,0:T(8,128)S(1)} custom-call(f32[1,128,128]{2,1,0:T(8,128)S(1)} %get-tuple-element.21), custom_call_target="InvertDiagBlocksLowerTriangular" | custom-call | tf_op jit(solution)/shard_map/triangular_solve | solution.py:41
  369.2 2.9 convolution_convert_fusion
  372.1 3.5 all-to-all-start.1
  376.3 14.2 %all-to-all-done.1 = bf16[4,32,4096]{2,1,0:T(8,128)(2,1)S(1)} async-done(((bf16[4,32,4096]{2,1,0:T(8,128)(2,1)}), bf16[4,32,4096]{2,1,0:T(8,128)(2,1)S(1)}, u32[]{:S(2)}, u32[]{:S(2)}) %all-to-all-start.1) | async-done | bytes 1048608 | tf_op jit(solution)/shard_map/all_to_all | solution.py:75
  (36 shorter events, 17.4 us)
Async XLA Ops:
  7.2 337.1 %all-reduce.6.cloned.1.call-start = ((), (), s32[]{:S(2)}) async-start(), calls=%async_computation.2 | async-start | bytes 131072 | tf_op jit(solution)/shard_map/psum | solution.py:69
  9.1 7.8 %collective-permute-start = (f32[32,1,2048]{2,0,1:T(8,128)S(1)}, f32[32,1,2048]{2,0,1:T(8,128)S(1)}, u32[]{:S(2)}, u32[]{:S(2)}) collective-permute-start(f32[32,1,2048]{2,0,1:T(8,128)S(1)} %get-tuple-element.18), channel_id=1, source_target_pairs={{0,4},{4,8},{8,12},{12,16},{16,20},{20,24},{24,28},{28,32},{32,36}... | collective-permute-start | bytes 786440 | tf_op jit(solution)/shard_map/ppermute | solution.py:12
  13.6 8.6 %copy-start.1 = (f32[8,2048]{1,0:T(8,128)S(1)}, f32[8,2048]{1,0:T(8,128)}, u32[]{:S(2)}) copy-start(f32[8,2048]{1,0:T(8,128)} %param.6) | copy-start | bytes 196612
  13.6 7.8 %collective-permute-start.1 = (f32[32,1,2048]{2,0,1:T(8,128)S(1)}, f32[32,1,2048]{2,0,1:T(8,128)S(1)}, u32[]{:S(2)}, u32[]{:S(2)}) collective-permute-start(f32[32,1,2048]{2,0,1:T(8,128)S(1)} %get-tuple-element.19), channel_id=1, source_target_pairs={{4,0},{8,4},{12,8},{16,12},{20,16},{24,20},{28,24},{32,28},{36,32}... | collective-permute-start | bytes 786440 | tf_op jit(solution)/shard_map/ppermute | solution.py:15
  22.2 5.4 %copy-start.2 = (f32[8,2048]{1,0:T(8,128)S(1)}, f32[8,2048]{1,0:T(8,128)}, u32[]{:S(2)}) copy-start(f32[8,2048]{1,0:T(8,128)} %param.5) | copy-start | bytes 196612
  23.3 5.2 %collective-permute-start.2 = (f32[32,1,2048]{2,0,1:T(8,128)S(1)}, f32[32,1,2048]{2,0,1:T(8,128)S(1)}, u32[]{:S(2)}, u32[]{:S(2)}) collective-permute-start(f32[32,1,2048]{2,0,1:T(8,128)S(1)} %get-tuple-element.16), channel_id=1, source_target_pairs={{0,4},{4,8},{8,12},{12,16},{16,20},{20,24},{24,28},{28,32},{32,36}... | collective-permute-start | bytes 786440 | tf_op jit(solution)/shard_map/ppermute | solution.py:12
  25.2 7.7 %collective-permute-start.3 = (f32[32,1,2048]{2,0,1:T(8,128)S(1)}, f32[32,1,2048]{2,0,1:T(8,128)S(1)}, u32[]{:S(2)}, u32[]{:S(2)}) collective-permute-start(f32[32,1,2048]{2,0,1:T(8,128)S(1)} %get-tuple-element.17), channel_id=1, source_target_pairs={{4,0},{8,4},{12,8},{16,12},{20,16},{24,20},{28,24},{32,28},{36,32}... | collective-permute-start | bytes 786440 | tf_op jit(solution)/shard_map/ppermute | solution.py:15
  27.7 6.0 %copy-start.3 = (f32[8,2048]{1,0:T(8,128)S(1)}, f32[8,2048]{1,0:T(8,128)}, u32[]{:S(2)}) copy-start(f32[8,2048]{1,0:T(8,128)} %param.7) | copy-start | bytes 196612
  35.3 5.2 %collective-permute-start.4 = (f32[32,1,2048]{2,0,1:T(8,128)S(1)}, f32[32,1,2048]{2,0,1:T(8,128)S(1)}, u32[]{:S(2)}, u32[]{:S(2)}) collective-permute-start(f32[32,1,2048]{2,0,1:T(8,128)S(1)} %get-tuple-element.14), channel_id=1, source_target_pairs={{0,4},{4,8},{8,12},{12,16},{16,20},{20,24},{24,28},{28,32},{32,36}... | collective-permute-start | bytes 786440 | tf_op jit(solution)/shard_map/ppermute | solution.py:12
  37.2 7.7 %collective-permute-start.5 = (f32[32,1,2048]{2,0,1:T(8,128)S(1)}, f32[32,1,2048]{2,0,1:T(8,128)S(1)}, u32[]{:S(2)}, u32[]{:S(2)}) collective-permute-start(f32[32,1,2048]{2,0,1:T(8,128)S(1)} %get-tuple-element.15), channel_id=1, source_target_pairs={{4,0},{8,4},{12,8},{16,12},{20,16},{24,20},{28,24},{32,28},{36,32}... | collective-permute-start | bytes 786440 | tf_op jit(solution)/shard_map/ppermute | solution.py:15
  46.7 5.2 %collective-permute-start.6 = (f32[32,1,2048]{2,0,1:T(8,128)S(1)}, f32[32,1,2048]{2,0,1:T(8,128)S(1)}, u32[]{:S(2)}, u32[]{:S(2)}) collective-permute-start(f32[32,1,2048]{2,0,1:T(8,128)S(1)} %get-tuple-element.12), channel_id=1, source_target_pairs={{0,4},{4,8},{8,12},{12,16},{16,20},{20,24},{24,28},{28,32},{32,36}... | collective-permute-start | bytes 786440 | tf_op jit(solution)/shard_map/ppermute | solution.py:12
  48.6 10.4 %copy-start = (bf16[32,8,2048]{2,1,0:T(8,128)(2,1)S(1)}, bf16[32,8,2048]{2,1,0:T(8,128)(2,1)}, u32[]{:S(2)}) copy-start(bf16[32,8,2048]{2,1,0:T(8,128)(2,1)} %param.4) | copy-start | bytes 3145732
  48.6 9.6 %collective-permute-start.7 = (f32[32,1,2048]{2,0,1:T(8,128)S(1)}, f32[32,1,2048]{2,0,1:T(8,128)S(1)}, u32[]{:S(2)}, u32[]{:S(2)}) collective-permute-start(f32[32,1,2048]{2,0,1:T(8,128)S(1)} %get-tuple-element.13), channel_id=1, source_target_pairs={{4,0},{8,4},{12,8},{16,12},{20,16},{24,20},{28,24},{32,28},{36,32}... | collective-permute-start | bytes 786440 | tf_op jit(solution)/shard_map/ppermute | solution.py:15
  372.1 18.5 %all-to-all-start.1 = ((bf16[4,32,4096]{2,1,0:T(8,128)(2,1)}), bf16[4,32,4096]{2,1,0:T(8,128)(2,1)S(1)}, u32[]{:S(2)}, u32[]{:S(2)}) async-start(bf16[4,32,4096]{2,1,0:T(8,128)(2,1)} %bitcast.5), calls=%async_computation.1 | async-start | bytes 2097152 | tf_op jit(solution)/shard_map/all_to_all | solution.py:75
Sparse Core Ops, SparseCore 0:
  94.7 249.5 all-reduce.5
where the time goes:
time: 400 us; the launch traced here: 399 us
  waiting for transfers between devices  287 us (72%)
  other arithmetic  33.3 us (8%)
  blocking collectives  25.8 us (6%)
  starting transfers between devices  23.3 us (6%)
  between operations  14.3 us (4%)
  local copies, waits for them, and re-layouts  9.82 us (2%)
  matrix products  5.55 us (1%)
    psum x1, waiting for transfers between devices, per_device(): gram_total = lax.psum(partial_gram, ('space', 'dir'))  250 us
    all_to_all x1, blocking collectives, per_device(): lax.all_to_all(flat, 'dir', split_axis=1, concat_axis=0, tiled=True)  25.8 us
    ppermute x4, waiting for transfers between devices, with_halo(): lax.ppermute(lax.slice_in_dim(block, 0, width, axis=dim), axis, backward)  19.6 us
    all_to_all x1, waiting for transfers between devices, per_device(): lax.all_to_all(basis_rows.astype(jnp.bfloat16), 'dir', split_axis=0, conc...  14.2 us
    another operation x3, other arithmetic, per_device(): lower_factor = jnp.linalg.cholesky(gram_total)  12.4 us
    ppermute x4, starting transfers between devices, with_halo(): lax.ppermute(lax.slice_in_dim(block, block.shape[dim] - width, None, axis...  10.3 us
    another operation x1, other arithmetic, invert_lower(): lax.linalg.triangular_solve(lower_factor, jnp.eye(width, dtype=jnp.float3...  9.81 us
    ppermute x4, starting transfers between devices, with_halo(): lax.ppermute(lax.slice_in_dim(block, 0, width, axis=dim), axis, backward)  9.46 us
  transfers between devices with their start and end apart: 10, of which 10 were waited for; matrix products, arithmetic and copies ran while one was open for 0% of the time, Pallas kernels for 0%

commit v1 on v0

v1 whole, which is shorter than its diff:
```python
import functools

import jax
import jax.numpy as jnp
from jax import lax
from jax.experimental import pallas as pl
from jax.experimental.pallas import tpu as pltpu
from jax.sharding import PartitionSpec as P

MESH = pl.DeviceIdType.MESH
F32 = jnp.float32
BF16 = jnp.bfloat16
HALO = 4


def nt_dot(a, b):
    return lax.dot_general(a, b, (((1,), (1,)), ((), ())), preferred_element_type=F32)


def nn_dot(a, b):
    return lax.dot_general(a, b, (((1,), (0,)), ((), ())), preferred_element_type=F32)


def split(x):
    high = x.astype(BF16)
    return high, (x - high.astype(F32)).astype(BF16)


def factor_and_inverse(gram):
    size = gram.shape[0]
    tiles = size // 8
    eye = (lax.broadcasted_iota(jnp.int32, (size, size), 0) == lax.broadcasted_iota(jnp.int32, (size, size), 1)).astype(F32)
    left = [gram[8 * t : 8 * t + 8] for t in range(tiles)]
    right = [eye[8 * t : 8 * t + 8] for t in range(tiles)]
    sub = lax.broadcasted_iota(jnp.int32, (8, 1), 0)
    for k in range(size):
        p, i = divmod(k, 8)
        scale = lax.rsqrt(left[p][i : i + 1, k : k + 1])
        row_left = left[p][i : i + 1] * scale
        row_right = right[p][i : i + 1] * scale
        for t in range(p, tiles):
            col = left[t][:, k : k + 1] * scale
            if t == p:
                here = sub == i
                col = jnp.where(sub > i, col, 0.0)
                left[t] = jnp.where(here, row_left, left[t] - col * row_left)
                right[t] = jnp.where(here, row_right, right[t] - col * row_right)
            else:
                left[t] = left[t] - col * row_left
                right[t] = right[t] - col * row_right
    upper = jnp.concatenate(left, axis=0)
    keep = lax.broadcasted_iota(jnp.int32, (size, size), 0) <= lax.broadcasted_iota(jnp.int32, (size, size), 1)
    return jnp.where(keep, upper, 0.0), jnp.concatenate(right, axis=0)


def sketch_kernel(
    cfg, dirs_ref, depth_ref, sens_ref, obs_ref, out_ref, factor_ref,
    turned, packs, main, halos, coef, coef_own, coef_in, both, gram, part, part_b, part_c, result,
    y_send, y_recv, s_send, s_recv, c_send, c_recv, g_send, g_recv, o_send, o_recv, own_sem,
):
    nd, ns, nx, nz, rows, cols, dirs, total_cells = cfg
    quarter = cols // nd
    wide = quarter + 128
    group = dirs // nd
    ext = rows + 2 * HALO
    na, nb = nx * nd, nz * 2
    tile = dirs // na

    s = lax.axis_index("space")
    d = lax.axis_index("dir")
    z, x, c = s // (2 * nx), (s // 2) % nx, s % 2
    ia = x * nd + d
    ib = z * 2 + c
    down, up = lax.rem(s + ns - 1, ns), lax.rem(s + 1, ns)

    def at_a(k):
        i = lax.rem(ia + k, na)
        return i, {"space": (z * nx + i // nd) * 2 + c, "dir": lax.rem(i, nd)}

    def at_b(k):
        i = lax.rem(ib + k, nb)
        return {"space": ((i // 2) * nx + x) * 2 + lax.rem(i, 2), "dir": d}

    barrier = pltpu.get_barrier_semaphore()
    peers = [{"space": s, "dir": lax.rem(d + k, nd)} for k in range(1, nd)]
    peers += [{"space": down, "dir": d}, {"space": up, "dir": d}]
    peers += [at_a(k)[1] for k in range(1, na)] + [at_b(k) for k in range(1, nb)]
    for peer in peers:
        pl.semaphore_signal(barrier, inc=1, device_id=peer, device_id_type=MESH)

    lane = lax.broadcasted_iota(jnp.int32, (1, 128), 1)
    edge = (lane < HALO) | (lane >= 128 - HALO)

    chunk = 256

    def turn(j, carry):
        here = pl.ds(pl.multiple_of(j * chunk, chunk), chunk)
        turned[:, :, here] = jnp.swapaxes(dirs_ref[:, :, here].astype(F32), 0, 1).astype(BF16)
        return carry

    lax.fori_loop(0, cols // chunk, turn, 0)

    for q in range(nd):
        packed = jnp.zeros((group, 128), F32)
        for r in range(rows):
            after = turned[r, :, (q + 1) * quarter : (q + 1) * quarter + 128].astype(F32) if q < nd - 1 else jnp.zeros((group, 128), F32)
            before = turned[r, :, q * quarter - 128 : q * quarter].astype(F32) if q > 0 else jnp.zeros((group, 128), F32)
            beside = jnp.where(lane < 64, after, before)
            packed = jnp.where((lane >= 8 * r) & (lane < 8 * r + 8), pltpu.roll(beside, 8 * r + HALO, 1), packed)
        packs[q] = packed.astype(BF16)

    inner = pl.ds(pl.multiple_of(d * quarter, 128), quarter)
    after = pl.ds(pl.multiple_of(jnp.minimum((d + 1) * quarter, cols - 128), 128), 128)
    before = pl.ds(pl.multiple_of(jnp.maximum(d * quarter - 128, 0), 128), 128)
    valid = ((lane < HALO) & (d < nd - 1)) | ((lane >= 128 - HALO) & (d > 0))

    def quarter_of(ref):
        return jnp.concatenate([ref[:, inner], jnp.where(lane < 64, ref[:, after], ref[:, before])], axis=1)

    inside = jnp.concatenate([jnp.ones((1, quarter), jnp.bool_), valid], axis=1)
    depth = quarter_of(depth_ref)
    coef_own[0] = jnp.where(inside, 0.1 * quarter_of(sens_ref), 0.0)
    coef_own[1] = jnp.where(inside, 20.0 / depth - 4.0, 0.0)
    coef_own[2] = jnp.where(inside, 0.1 * depth * depth * quarter_of(obs_ref), 0.0)

    pl.semaphore_wait(barrier, len(peers))

    coef_copies = []
    for side, peer in enumerate((up, down)):
        copy = pltpu.make_async_remote_copy(
            src_ref=coef_own, dst_ref=coef_in.at[side], send_sem=c_send.at[side], recv_sem=c_recv.at[side],
            device_id={"space": peer, "dir": d}, device_id_type=MESH)
        copy.start()
        coef_copies.append(copy)

    def dirs_at(g):
        return pl.ds(pl.multiple_of(g * group, group), group)

    def cols_at(q):
        return pl.ds(pl.multiple_of(q * quarter, 128), quarter)

    own_main = pltpu.make_async_copy(turned.at[:, :, cols_at(d)], main.at[pl.ds(HALO, rows), dirs_at(d), :], own_sem.at[0])
    own_pack = pltpu.make_async_copy(packs.at[d], halos.at[1, dirs_at(d), :], own_sem.at[1])
    own_main.start()
    own_pack.start()

    y_copies = {}
    for k in [1, nd - 1] + list(range(2, nd - 1)):
        if k in y_copies:
            continue
        q = lax.rem(d + k, nd)
        peer = {"space": s, "dir": q}
        copies = (
            pltpu.make_async_remote_copy(
                src_ref=turned.at[:, :, cols_at(q)], dst_ref=main.at[pl.ds(HALO, rows), dirs_at(d), :],
                send_sem=y_send.at[0, k], recv_sem=y_recv.at[0, k], device_id=peer, device_id_type=MESH),
            pltpu.make_async_remote_copy(
                src_ref=packs.at[q], dst_ref=halos.at[1, dirs_at(d), :],
                send_sem=y_send.at[1, k], recv_sem=y_recv.at[1, k], device_id=peer, device_id_type=MESH),
        )
        for copy in copies:
            copy.start()
        y_copies[k] = copies

    own_main.wait()
    own_pack.wait()

    def send_rows(k):
        g = lax.rem(d + nd - k, nd)
        copies = []
        for side, peer in enumerate((up, down)):
            source = pl.ds(rows, HALO) if side == 0 else pl.ds(HALO, HALO)
            target = pl.ds(0, HALO) if side == 0 else pl.ds(HALO + rows, HALO)
            for sort, (src, dst) in enumerate((
                (main.at[source, dirs_at(g), :], main.at[target, dirs_at(g), :]),
                (halos.at[1, dirs_at(g), :], halos.at[2 * side, dirs_at(g), :]),
            )):
                copy = pltpu.make_async_remote_copy(
                    src_ref=src, dst_ref=dst, send_sem=s_send.at[sort, side, k], recv_sem=s_recv.at[sort, side, k],
                    device_id={"space": peer, "dir": d}, device_id_type=MESH)
                copy.start()
                copies.append(copy)
        return copies

    row_copies = {0: send_rows(0)}

    for copy in coef_copies:
        copy.wait()
    for i in range(3):
        coef[i, HALO : HALO + rows] = coef_own[i]
        coef[i, 0:HALO] = jnp.where(s > 0, coef_in[0, i, rows - HALO : rows], 0.0)
        coef[i, HALO + rows : ext] = jnp.where(s < ns - 1, coef_in[1, i, 0:HALO], 0.0)

    block = 16

    def stencil(base):
        here = pl.ds(pl.multiple_of(base, block), block)

        def raw(e):
            if e < HALO:
                side, r = 0, rows - HALO + e
            elif e < HALO + rows:
                side, r = 1, e - HALO
            else:
                side, r = 2, e - HALO - rows
            beside = pltpu.roll(halos[side, here, :].astype(F32), (128 - 8 * r - HALO) % 128, 1)
            row = jnp.concatenate([main[e, here, :].astype(F32), jnp.where(edge, beside, 0.0)], axis=1)
            if side == 0:
                row = jnp.where(s > 0, row, 0.0)
            if side == 2:
                row = jnp.where(s < ns - 1, row, 0.0)
            return row

        def around(above, row, below):
            return (above + below) + (pltpu.roll(row, 1, 1) + pltpu.roll(row, wide - 1, 1))

        field, state, flux, source = {}, {}, {}, {}
        for e in range(ext):
            field[e] = raw(e)
            j = e - 1
            if j >= 1:
                state[j] = coef[0, j : j + 1] * (around(field[j - 1], field[j], field[j + 1]) + 6.0 * field[j])
            j = e - 2
            if j >= 2:
                flux[j] = coef[2, j : j + 1] * (around(state[j - 1], state[j], state[j + 1]) + coef[1, j : j + 1] * state[j])
            j = e - 3
            if j >= 3:
                source[j] = coef[0, j : j + 1] * (around(flux[j - 1], flux[j], flux[j + 1]) + coef[1, j : j + 1] * flux[j])
            j = e - 4
            if j >= 4:
                value = field[j] + 0.1 * (around(source[j - 1], source[j], source[j + 1]) + 6.0 * source[j])
                high, low = split(value[:, :quarter])
                both[j - HALO, here, :] = high
                both[j - HALO, pl.ds(pl.multiple_of(dirs + base, block), block), :] = low

    def stencil_group(k):
        g = lax.rem(d + nd - k, nd)

        def step(j, carry):
            stencil(g * group + j * block)
            return carry

        lax.fori_loop(0, group // block, step, 0)

    def wait_y(k):
        for copy in y_copies[k]:
            copy.wait_recv()

    def wait_rows(k):
        for copy in row_copies[k]:
            copy.wait_recv()

    order = list(y_copies)
    wait_rows(0)
    stencil_group(0)
    wait_y(order[0])
    row_copies[order[0]] = send_rows(order[0])
    for n, k in enumerate(order):
        if n + 1 < len(order):
            wait_y(order[n + 1])
            row_copies[order[n + 1]] = send_rows(order[n + 1])
        wait_rows(k)
        stencil_group(k)

    gram[...] = jnp.zeros_like(gram)

    def gram_step(r, carry):
        gram[...] += nt_dot(both[r], both[r])
        return carry

    lax.fori_loop(0, rows, gram_step, 0)
    mixed = gram[0:dirs, dirs : 2 * dirs] + gram[dirs : 2 * dirs, 0:dirs]
    local = (gram[0:dirs, 0:dirs] + gram[dirs : 2 * dirs, dirs : 2 * dirs] + mixed) * (1.0 / total_cells)
    result[...] = local.reshape(na, tile, dirs)

    def all_of(ref, count, sem):
        return pltpu.make_async_copy(ref.at[pl.ds(0, count)], ref.at[pl.ds(0, count)], sem)

    for k in range(1, na):
        i, peer = at_a(k)
        pltpu.make_async_remote_copy(
            src_ref=result.at[i], dst_ref=part.at[ia], send_sem=g_send.at[0], recv_sem=g_recv.at[0],
            device_id=peer, device_id_type=MESH).start()
    part[ia] = result[ia]
    all_of(part, na - 1, g_recv.at[0]).wait()
    part_b[ib] = jnp.sum(part[...], axis=0)
    for k in range(1, nb):
        pltpu.make_async_remote_copy(
            src_ref=part_b.at[ib], dst_ref=part_b.at[ib], send_sem=g_send.at[1], recv_sem=g_recv.at[1],
            device_id=at_b(k), device_id_type=MESH).start()
    all_of(part_b, nb - 1, g_recv.at[1]).wait()
    part_c[ia] = jnp.sum(part_b[...], axis=0)
    for k in range(1, na):
        pltpu.make_async_remote_copy(
            src_ref=part_c.at[ia], dst_ref=part_c.at[ia], send_sem=g_send.at[2], recv_sem=g_recv.at[2],
            device_id=at_a(k)[1], device_id_type=MESH).start()
    all_of(part_c, na - 1, g_recv.at[2]).wait()

    upper, inverse = factor_and_inverse(part_c[...].reshape(dirs, dirs))
    factor_ref[...] = upper
    inverse_high, inverse_low = split(inverse)
    inverse_twice = jnp.concatenate([inverse_high, inverse_high], axis=1)

    step_rows = 2

    def basis_step(j, carry):
        for t in range(step_rows):
            r = j * step_rows + t
            value = nn_dot(inverse_twice, both[r]) + nn_dot(inverse_low, both[r, 0:dirs, :])
            turned_out[r] = value.astype(BF16)
        for k in range(1, nd):
            q = lax.rem(d + k, nd)
            here = pl.ds(j * step_rows, step_rows)
            pltpu.make_async_remote_copy(
                src_ref=turned_out.at[here, dirs_at(q), :], dst_ref=out_ref.at[here, :, cols_at(d)],
                send_sem=o_send.at[0], recv_sem=o_recv.at[0],
                device_id={"space": s, "dir": q}, device_id_type=MESH).start()
        return carry

    turned_out = main.at[pl.ds(0, rows)]
    for copies in row_copies.values():
        for copy in copies:
            copy.wait_send()
    lax.fori_loop(0, rows // step_rows, basis_step, 0)
    out_ref[:, :, cols_at(d)] = turned_out[:, dirs_at(d), :]
    away = pl.ds(0, (nd - 1) * quarter)
    pltpu.make_async_copy(out_ref.at[:, :, away], out_ref.at[:, :, away], o_recv.at[0]).wait()

    for copies in y_copies.values():
        for copy in copies:
            copy.wait_send()
    all_of(part, na - 1, g_send.at[0]).wait()
    all_of(part_b, nb - 1, g_send.at[1]).wait()
    all_of(part_c, na - 1, g_send.at[2]).wait()
    pltpu.make_async_copy(out_ref.at[:, :, away], out_ref.at[:, :, away], o_send.at[0]).wait()


def order_kernel(in_ref, factor_in, out_ref, factor_out):
    chunk = 256

    def turn(j, carry):
        here = pl.ds(pl.multiple_of(j * chunk, chunk), chunk)
        out_ref[:, :, here] = jnp.swapaxes(in_ref[:, :, here].astype(F32), 0, 1).astype(BF16)
        return carry

    lax.fori_loop(0, in_ref.shape[2] // chunk, turn, 0)
    factor_out[...] = factor_in[...]


def per_device(ns, nd, directions, depth_coef, sensitivity, obs_weight):
    group, rows, cols = directions.shape
    dirs = group * nd
    nx = 4 if ns >= 8 else ns // 2
    nz = ns // (2 * nx)
    na, nb = nx * nd, nz * 2
    tile = dirs // na
    quarter = cols // nd
    wide = quarter + 128
    ext = rows + 2 * HALO
    cfg = (nd, ns, nx, nz, rows, cols, dirs, rows * ns * cols)
    vmem = pl.BlockSpec(memory_space=pltpu.VMEM)
    dma = pltpu.SemaphoreType.DMA
    turned, factor = pl.pallas_call(
        functools.partial(sketch_kernel, cfg),
        out_shape=(jax.ShapeDtypeStruct((rows, group, cols), BF16), jax.ShapeDtypeStruct((dirs, dirs), F32)),
        in_specs=[vmem] * 4,
        out_specs=(vmem, vmem),
        scratch_shapes=[
            pltpu.VMEM((rows, group, cols), BF16),
            pltpu.VMEM((nd, group, 128), BF16),
            pltpu.VMEM((ext, dirs, quarter), BF16),
            pltpu.VMEM((3, dirs, 128), BF16),
            pltpu.VMEM((3, ext, wide), F32),
            pltpu.VMEM((3, rows, wide), F32),
            pltpu.VMEM((2, 3, rows, wide), F32),
            pltpu.VMEM((rows, 2 * dirs, quarter), BF16),
            pltpu.VMEM((2 * dirs, 2 * dirs), F32),
            pltpu.VMEM((na, tile, dirs), F32),
            pltpu.VMEM((nb, tile, dirs), F32),
            pltpu.VMEM((na, tile, dirs), F32),
            pltpu.VMEM((na, tile, dirs), F32),
            dma((2, nd)), dma((2, nd)), dma((2, 2, nd)), dma((2, 2, nd)), dma((2,)), dma((2,)),
            dma((3,)), dma((3,)), dma((1,)), dma((1,)), dma((2,)),
        ],
        compiler_params=pltpu.CompilerParams(collective_id=0, has_side_effects=True, vmem_limit_bytes=40 * 2**20),
    )(directions, depth_coef, sensitivity, obs_weight)
    return pl.pallas_call(
        order_kernel,
        out_shape=(jax.ShapeDtypeStruct((group, rows, cols), BF16), jax.ShapeDtypeStruct((dirs, dirs), F32)),
        in_specs=[vmem] * 2,
        out_specs=(vmem, vmem),
        compiler_params=pltpu.CompilerParams(vmem_limit_bytes=40 * 2**20),
    )(turned, factor)


def solution(mesh):
    return jax.shard_map(
        functools.partial(per_device, mesh.shape["space"], mesh.shape["dir"]),
        mesh=mesh,
        in_specs=(P("dir", "space", None), P("space", None), P("space", None), P("space", None)),
        out_specs=(P("dir", "space", None), P()),
        check_vma=False,
    )
```

time: 400 us -> 80.8 us (0.20)
  waiting for transfers between devices: 287 us -> 0 us
  Pallas kernels: 0 us -> 76.1 us
  other arithmetic: 33.3 us -> 0 us
  blocking collectives: 25.8 us -> 0 us
  starting transfers between devices: 23.3 us -> 0 us
  between operations: 14.3 us -> 0.65 us
  local copies, waits for them, and re-layouts: 9.82 us -> 3.73 us
  matrix products: 5.55 us -> 0 us
    psum x1 -> x0, waiting for transfers between devices: 250 us -> none  [per_device(): gram_total = lax.psum(partial_gram, ('space', 'dir'))]
    pallas_call x0 -> x2, Pallas kernels: none -> 76.1 us  [the longest x1 74.7 us: per_device(): pl.pallas_call(functools.partial(sketch_kernel, cfg), out_shape=(jax.Shap...]
    all_to_all x1 -> x0, blocking collectives: 25.8 us -> none  [per_device(): lax.all_to_all(flat, 'dir', split_axis=1, concat_axis=0, tiled=True)]
    ppermute x8 -> x0, waiting for transfers between devices: 23.2 us -> none  [the longest x4 19.6 us: with_halo(): lax.ppermute(lax.slice_in_dim(block, 0, width, axis=dim), axis, backward)]
    another operation x4 -> x0, other arithmetic: 22.2 us -> none  [the longest x3 12.4 us: per_device(): lower_factor = jnp.linalg.cholesky(gram_total)]
    ppermute x8 -> x0, starting transfers between devices: 19.7 us -> none  [the longest x4 10.3 us: with_halo(): lax.ppermute(lax.slice_in_dim(block, block.shape[dim] - width, None, axis...]
    all_to_all x1 -> x0, waiting for transfers between devices: 14.2 us -> none  [per_device(): lax.all_to_all(basis_rows.astype(jnp.bfloat16), 'dir', split_axis=0, conc...]
    all_to_all x3 -> x0, local copies, waits for them, and re-layouts: 5.67 us -> none  [the longest x2 4.86 us: per_device(): lax.all_to_all(flat, 'dir', split_axis=1, concat_axis=0, tiled=True)]
  transfers between devices with their start and end apart: 10 -> 0, of which waited for: 10 -> 0; matrix products, arithmetic and copies ran while one was open for 0% -> 0% of each run, Pallas kernels for 0% -> 0%
where the time goes in v1:
time: 80.8 us; the launch traced here: 80.5 us
  Pallas kernels  76.1 us (94%)
  local copies, waits for them, and re-layouts  3.73 us (5%)
    pallas_call x1, Pallas kernels, per_device(): pl.pallas_call(functools.partial(sketch_kernel, cfg), out_shape=(jax.Shap...  74.7 us
    unnamed x8, local copies, waits for them, and re-layouts  3.73 us

profile of v1, /device:TPU:1, one launch (start us, length us, event | category | flops | bytes accessed | tf_op | source)
XLA Modules:
  0.0 80.5 jit_solution(17035801020738427719)
XLA Ops:
  0.6 0.0 copy-start
  0.6 1.2 %copy-done = bf16[32,8,2048]{2,1,0:T(8,128)(2,1)S(1)} copy-done((bf16[32,8,2048]{2,1,0:T(8,128)(2,1)S(1)}, bf16[32,8,2048]{2,1,0:T(8,128)(2,1)}, u32[]{:S(2)}) %copy-start) | copy-done | bytes 1048600
  1.9 0.0 copy-start.1
  1.9 0.8 %copy-done.1 = f32[8,2048]{1,0:T(8,128)S(1)} copy-done((f32[8,2048]{1,0:T(8,128)S(1)}, f32[8,2048]{1,0:T(8,128)}, u32[]{:S(2)}) %copy-start.1) | copy-done | bytes 65560
  2.7 0.0 copy-start.2
  2.7 0.8 %copy-done.2 = f32[8,2048]{1,0:T(8,128)S(1)} copy-done((f32[8,2048]{1,0:T(8,128)S(1)}, f32[8,2048]{1,0:T(8,128)}, u32[]{:S(2)}) %copy-start.2) | copy-done | bytes 65560
  3.5 0.0 copy-start.3
  3.5 0.8 %copy-done.3 = f32[8,2048]{1,0:T(8,128)S(1)} copy-done((f32[8,2048]{1,0:T(8,128)S(1)}, f32[8,2048]{1,0:T(8,128)}, u32[]{:S(2)}) %copy-start.3) | copy-done | bytes 65560
  4.4 74.7 %shard_map.59 = (bf16[8,32,2048]{2,1,0:T(8,128)(2,1)S(1)}, f32[128,128]{1,0:T(8,128)S(1)}) custom-call(bf16[32,8,2048]{2,1,0:T(8,128)(2,1)S(1)} %copy-done, f32[8,2048]{1,0:T(8,128)S(1)} %copy-done.1, f32[8,2048]{1,0:T(8,128)S(1)} %copy-done.2, f32[8,2048]{1,0:T(8,128)S(1)} %copy-done.3), custom_call_target="tpu_custom_call" | custom-call | tf_op jit(solution)/shard_map/pallas_call | solution.py:363
  79.0 1.5 %shard_map.60 = (bf16[32,8,2048]{2,1,0:T(8,128)(2,1)}, f32[128,128]{1,0:T(8,128)}) custom-call(bf16[8,32,2048]{2,1,0:T(8,128)(2,1)S(1)} %get-tuple-element.4.in_ref, f32[128,128]{1,0:T(8,128)S(1)} %get-tuple-element.5.factor_in), custom_call_target="tpu_custom_call" | custom-call | tf_op jit(solution)/shard_map/pallas_call | solution.py:387
Async XLA Ops:
  0.6 1.2 %copy-start = (bf16[32,8,2048]{2,1,0:T(8,128)(2,1)S(1)}, bf16[32,8,2048]{2,1,0:T(8,128)(2,1)}, u32[]{:S(2)}) copy-start(bf16[32,8,2048]{2,1,0:T(8,128)(2,1)} %dirs_ref.1) | copy-start | bytes 3145732
  1.9 0.8 %copy-start.1 = (f32[8,2048]{1,0:T(8,128)S(1)}, f32[8,2048]{1,0:T(8,128)}, u32[]{:S(2)}) copy-start(f32[8,2048]{1,0:T(8,128)} %depth_ref.1) | copy-start | bytes 196612
  2.7 0.8 %copy-start.2 = (f32[8,2048]{1,0:T(8,128)S(1)}, f32[8,2048]{1,0:T(8,128)}, u32[]{:S(2)}) copy-start(f32[8,2048]{1,0:T(8,128)} %sens_ref.1) | copy-start | bytes 196612
  3.5 0.8 %copy-start.3 = (f32[8,2048]{1,0:T(8,128)S(1)}, f32[8,2048]{1,0:T(8,128)}, u32[]{:S(2)}) copy-start(f32[8,2048]{1,0:T(8,128)} %obs_ref.1) | copy-start | bytes 196612

commit v2 on v1

v2 whole, which is shorter than its diff:
```python
import functools

import jax
import jax.numpy as jnp
from jax import lax
from jax.experimental import pallas as pl
from jax.experimental.pallas import tpu as pltpu
from jax.sharding import PartitionSpec as P

MESH = pl.DeviceIdType.MESH
F32 = jnp.float32
BF16 = jnp.bfloat16
HALO = 4


def nt_dot(a, b):
    return lax.dot_general(a, b, (((1,), (1,)), ((), ())), preferred_element_type=F32)


def nn_dot(a, b):
    return lax.dot_general(a, b, (((1,), (0,)), ((), ())), preferred_element_type=F32)


def split(x):
    high = x.astype(BF16)
    return high, (x - high.astype(F32)).astype(BF16)


def tree_sum(terms):
    terms = list(terms)
    while len(terms) > 1:
        terms = [terms[i] + terms[i + 1] if i + 1 < len(terms) else terms[i] for i in range(0, len(terms), 2)]
    return terms[0]


def factor_and_inverse(tiles):
    size = 8 * len(tiles)
    tiles = list(tiles)

    def spread(v):
        return jnp.broadcast_to(v, (8, size))

    lane = lax.broadcasted_iota(jnp.int32, (8, size), 1)
    sub = lax.broadcasted_iota(jnp.int32, (8, size), 0)
    upper, inverse = [], []
    for p in range(len(tiles)):
        x, o = tiles[p], 8 * p
        columns = [spread(x[:, o + j : o + j + 1]) for j in range(8)]
        e = {(i, j): spread(columns[j][i : i + 1]) for j in range(8) for i in range(j, 8)}
        r, l, w, q = [], {}, {}, {}
        for j in range(8):
            r.append(lax.rsqrt(e[j, j]))
            for i in range(j + 1, 8):
                l[i, j] = e[i, j] * r[j]
            for i in range(j + 1, 8):
                for k in range(j + 1, i + 1):
                    e[i, k] = e[i, k] - l[i, j] * l[k, j]
        for j in range(8):
            w[j, j] = r[j]
            for i in range(j + 1, 8):
                w[i, j] = -r[i] * tree_sum([l[i, k] * w[k, j] for k in range(j, i)])
        for i in range(8):
            for j in range(i, 8):
                q[i, j] = q[j, i] = tree_sum([w[k, i] * w[k, j] for k in range(j, 8)])
        panel = (lane >= o) & (lane < o + 8)
        rows = [spread(v) for v in jnp.split(jnp.where(panel, jnp.where(lane - o == sub, 1.0, 0.0), x), 8, axis=0)]
        scaled = [tree_sum([q[i, j] * rows[j] for j in range(8)]) for i in range(8)]
        for t in range(p + 1, len(tiles)):
            taken = tree_sum([spread(tiles[t][:, o + j : o + j + 1]) * scaled[j] for j in range(8)])
            tiles[t] = jnp.where(panel, 0.0, tiles[t]) - taken
        weights = []
        for j in range(8):
            column = jnp.where(sub == j, w[j, j], 0.0)
            for i in range(j + 1, 8):
                column = jnp.where(sub == i, w[i, j], column)
            weights.append(column)
        below = tree_sum([weights[j] * rows[j] for j in range(8)])
        above = tree_sum([weights[j] * spread(x[j : j + 1]) for j in range(8)])
        inverse.append(jnp.where(lane < o + 8, below, 0.0))
        upper.append(jnp.where(lane >= o + sub, above, 0.0))
    return jnp.concatenate(upper, axis=0), jnp.concatenate(inverse, axis=0)


def sketch_kernel(
    cfg, dirs_hbm, depth_hbm, sens_hbm, obs_hbm, out_ref, factor_ref,
    dirs_ref, depth_ref, sens_ref, obs_ref, turned, packs, main, halos, coef, coef_own, coef_in, both, gram, part, part_b, part_c, result,
    sends, y_recv, s_recv, pack_recv, own_recv, c_recv, g_recv, o_recv, own_sem, in_sem,
):
    nd, ns, nx, nz, rows, cols, dirs, total_cells = cfg
    quarter = cols // nd
    wide = quarter + 128
    group = dirs // nd
    ext = rows + 2 * HALO
    na, nb = nx * nd, nz * 2
    tile = dirs // na

    s = lax.axis_index("space")
    d = lax.axis_index("dir")
    z, x, c = s // (2 * nx), (s // 2) % nx, s % 2
    ia = x * nd + d
    ib = z * 2 + c
    down, up = lax.rem(s + ns - 1, ns), lax.rem(s + 1, ns)

    def far(offset, length):
        return min(offset, length - offset)

    off_a = sorted(((i, j) for i in range(nx) for j in range(nd)), key=lambda o: -far(o[0], nx) - far(o[1], nd))[:-1]
    off_b = sorted(((i, j) for i in range(nz) for j in range(2)), key=lambda o: -2 * far(o[0], nz) - o[1])[:-1]

    def at_a(offset):
        i, j = lax.rem(x + offset[0], nx), lax.rem(d + offset[1], nd)
        return i * nd + j, {"space": (z * nx + i) * 2 + c, "dir": j}

    def at_b(offset):
        return {"space": (lax.rem(z + offset[0], nz) * nx + x) * 2 + lax.rem(c + offset[1], 2), "dir": d}

    def send(source, target, number, arrival, peer):
        pltpu.make_async_remote_copy(
            src_ref=source, dst_ref=target, send_sem=sends.at[number], recv_sem=arrival,
            device_id=peer, device_id_type=MESH).start()

    def await_bytes(ref, sem):
        pltpu.make_async_copy(ref, ref, sem).wait()

    inputs = [
        pltpu.make_async_copy(source, target, in_sem.at[i])
        for i, (source, target) in enumerate(
            ((dirs_hbm, dirs_ref), (depth_hbm, depth_ref), (sens_hbm, sens_ref), (obs_hbm, obs_ref)))
    ]
    for copy in inputs:
        copy.start()

    barrier = pltpu.get_barrier_semaphore()
    peers = [{"space": s, "dir": lax.rem(d + k, nd)} for k in range(1, nd)]
    peers += [{"space": down, "dir": d}, {"space": up, "dir": d}]
    peers += [{"space": (z * nx + lax.rem(x + k, nx)) * 2 + c, "dir": d} for k in range(1, nx)]
    peers += [{"space": (lax.rem(z + k, nz) * nx + x) * 2 + c, "dir": d} for k in range(1, nz)]
    for peer in peers:
        pl.semaphore_signal(barrier, inc=1, device_id=peer, device_id_type=MESH)

    lane = lax.broadcasted_iota(jnp.int32, (1, 128), 1)
    edge = (lane < HALO) | (lane >= 128 - HALO)

    inputs[0].wait()
    chunk = 256

    def turn(j, carry):
        here = pl.ds(pl.multiple_of(j * chunk, chunk), chunk)
        turned[:, :, here] = jnp.swapaxes(dirs_ref[:, :, here].astype(F32), 0, 1).astype(BF16)
        return carry

    lax.fori_loop(0, cols // chunk, turn, 0)

    for q in range(nd):
        packed = jnp.zeros((group, 128), F32)
        for r in range(rows):
            after = turned[r, :, (q + 1) * quarter : (q + 1) * quarter + 128].astype(F32) if q < nd - 1 else jnp.zeros((group, 128), F32)
            before = turned[r, :, q * quarter - 128 : q * quarter].astype(F32) if q > 0 else jnp.zeros((group, 128), F32)
            beside = jnp.where(lane < 64, after, before)
            packed = jnp.where((lane >= 8 * r) & (lane < 8 * r + 8), pltpu.roll(beside, 8 * r + HALO, 1), packed)
        packs[q] = packed.astype(BF16)

    for copy in inputs[1:]:
        copy.wait()
    inner = pl.ds(pl.multiple_of(d * quarter, 128), quarter)
    after = pl.ds(pl.multiple_of(jnp.minimum((d + 1) * quarter, cols - 128), 128), 128)
    before = pl.ds(pl.multiple_of(jnp.maximum(d * quarter - 128, 0), 128), 128)
    valid = ((lane < HALO) & (d < nd - 1)) | ((lane >= 128 - HALO) & (d > 0))

    def quarter_of(ref):
        return jnp.concatenate([ref[:, inner], jnp.where(lane < 64, ref[:, after], ref[:, before])], axis=1)

    inside = jnp.concatenate([jnp.ones((1, quarter), jnp.bool_), valid], axis=1)
    depth = quarter_of(depth_ref)
    coef_own[0] = jnp.where(inside, 0.1 * quarter_of(sens_ref), 0.0)
    coef_own[1] = jnp.where(inside, 20.0 / depth - 4.0, 0.0)
    coef_own[2] = jnp.where(inside, 0.1 * depth * depth * quarter_of(obs_ref), 0.0)

    pl.semaphore_wait(barrier, len(peers))

    above, below = {"space": up, "dir": d}, {"space": down, "dir": d}
    block = 16
    halves = group // block
    parts = 2
    part_cols = quarter // parts

    def dirs_at(g):
        return pl.ds(pl.multiple_of(g * group, group), group)

    def cols_at(q):
        return pl.ds(pl.multiple_of(q * quarter, 128), quarter)

    def place(h, k, count=1):
        return pl.ds((h * nd + k) * block, count * block)

    own_copies = [pltpu.make_async_copy(packs.at[d], halos.at[1, 0], own_sem.at[0])]
    for h in range(halves):
        own_copies.append(pltpu.make_async_copy(
            turned.at[:, pl.ds(h * block, block), cols_at(d)], main.at[pl.ds(HALO, rows), place(h, 0), :], own_sem.at[1 + h]))
    for copy in own_copies:
        copy.start()
    for k in range(1, nd):
        q = lax.rem(d + k, nd)
        send(packs.at[q], halos.at[1, k], 0, pack_recv.at[0], {"space": s, "dir": q})
    for side, peer in enumerate((above, below)):
        send(coef_own, coef_in.at[side], 1, c_recv.at[0], peer)
    for h in range(halves):
        here = pl.ds(h * block, block)
        send(turned.at[pl.ds(rows - HALO, HALO), here, cols_at(d)], main.at[pl.ds(0, HALO), place(h, 0), :], 2, own_recv.at[0], above)
        send(turned.at[pl.ds(0, HALO), here, cols_at(d)], main.at[pl.ds(HALO + rows, HALO), place(h, 0), :], 2, own_recv.at[0], below)
    for h in range(halves):
        for p in range(parts):
            for k in list(range(2, nd)) + [1]:
                q = lax.rem(d + k, nd)
                there = pl.ds(pl.multiple_of(q * quarter + p * part_cols, 128), part_cols)
                send(turned.at[:, pl.ds(h * block, block), there],
                     main.at[pl.ds(HALO, rows), place(h, k), pl.ds(p * part_cols, part_cols)],
                     3, y_recv.at[h * parts + p], {"space": s, "dir": q})
    for copy in own_copies:
        copy.wait()

    await_bytes(coef_in, c_recv.at[0])
    for i in range(3):
        coef[i, HALO : HALO + rows] = coef_own[i]
        coef[i, 0:HALO] = jnp.where(s > 0, coef_in[0, i, rows - HALO : rows], 0.0)
        coef[i, HALO + rows : ext] = jnp.where(s < ns - 1, coef_in[1, i, 0:HALO], 0.0)

    await_bytes(halos.at[1, pl.ds(0, nd - 1)], pack_recv.at[0])
    for side, peer in enumerate((above, below)):
        send(halos.at[1], halos.at[2 * side], 4, pack_recv.at[1], peer)

    def forward(h, p):
        await_bytes(main.at[pl.ds(0, rows), pl.ds(0, (nd - 1) * block), pl.ds(0, part_cols)], y_recv.at[h * parts + p])
        here = place(h, 1, nd - 1)
        there = pl.ds(p * part_cols, part_cols)
        send(main.at[pl.ds(rows, HALO), here, there], main.at[pl.ds(0, HALO), here, there], 5, s_recv.at[h * parts + p], above)
        send(main.at[pl.ds(HALO, HALO), here, there], main.at[pl.ds(HALO + rows, HALO), here, there], 5, s_recv.at[h * parts + p], below)

    def await_rows(h, p):
        await_bytes(main.at[pl.ds(0, 2 * HALO), pl.ds(0, (nd - 1) * block), pl.ds(0, part_cols)], s_recv.at[h * parts + p])


    def stencil(h, k):
        held = pl.ds(pl.multiple_of((h * nd + k) * block, block), block)
        base = lax.rem(d + nd - k, nd) * group + h * block
        here = pl.ds(pl.multiple_of(base, block), block)

        def raw(e):
            if e < HALO:
                side, r = 0, rows - HALO + e
            elif e < HALO + rows:
                side, r = 1, e - HALO
            else:
                side, r = 2, e - HALO - rows
            beside = pltpu.roll(halos[side, k, h * block : (h + 1) * block, :].astype(F32), (128 - 8 * r - HALO) % 128, 1)
            row = jnp.concatenate([main[e, held, :].astype(F32), jnp.where(edge, beside, 0.0)], axis=1)
            if side == 0:
                row = jnp.where(s > 0, row, 0.0)
            if side == 2:
                row = jnp.where(s < ns - 1, row, 0.0)
            return row

        def around(above, row, below):
            return (above + below) + (pltpu.roll(row, 1, 1) + pltpu.roll(row, wide - 1, 1))

        field, state, flux, source = {}, {}, {}, {}
        for e in range(ext):
            field[e] = raw(e)
            j = e - 1
            if j >= 1:
                state[j] = coef[0, j : j + 1] * (around(field[j - 1], field[j], field[j + 1]) + 6.0 * field[j])
            j = e - 2
            if j >= 2:
                flux[j] = coef[2, j : j + 1] * (around(state[j - 1], state[j], state[j + 1]) + coef[1, j : j + 1] * state[j])
            j = e - 3
            if j >= 3:
                source[j] = coef[0, j : j + 1] * (around(flux[j - 1], flux[j], flux[j + 1]) + coef[1, j : j + 1] * flux[j])
            j = e - 4
            if j >= 4:
                value = field[j] + 0.1 * (around(source[j - 1], source[j], source[j + 1]) + 6.0 * source[j])
                high, low = split(value[:, :quarter])
                both[j - HALO, here, :] = high
                both[j - HALO, pl.ds(pl.multiple_of(dirs + base, block), block), :] = low

    def stencils(h, first, last):
        def step(k, carry):
            stencil(h, k)
            return carry

        lax.fori_loop(first, last, step, 0)

    stages = [(h, p) for h in range(halves) for p in range(parts)]
    forward(*stages[0])
    await_bytes(main.at[pl.ds(0, 2 * HALO), pl.ds(0, halves * block), :], own_recv.at[0])
    await_bytes(halos.at[pl.ds(0, 2)], pack_recv.at[1])
    stencils(0, 0, 1)
    forward(*stages[1])
    stencils(1, 0, 1)
    forward(*stages[2])
    for p in range(parts):
        await_rows(0, p)
    stencils(0, 1, 2)
    forward(*stages[3])
    stencils(0, 2, nd)
    for p in range(parts):
        await_rows(1, p)
    stencils(1, 1, nd)

    gram[...] = jnp.zeros_like(gram)

    def gram_step(r, carry):
        gram[...] += nt_dot(both[r], both[r])
        return carry

    lax.fori_loop(0, rows, gram_step, 0)
    mixed = gram[0:dirs, dirs : 2 * dirs] + gram[dirs : 2 * dirs, 0:dirs]
    local = (gram[0:dirs, 0:dirs] + gram[dirs : 2 * dirs, dirs : 2 * dirs] + mixed) * (1.0 / total_cells)
    result[...] = local.reshape(na, tile, dirs)

    for offset in off_a:
        i, peer = at_a(offset)
        send(result.at[i], part.at[ia], 6, g_recv.at[0], peer)
    part[ia] = result[ia]
    await_bytes(part.at[pl.ds(0, na - 1)], g_recv.at[0])
    part_b[ib] = jnp.sum(part[...], axis=0)
    for offset in off_b:
        send(part_b.at[ib], part_b.at[ib], 7, g_recv.at[1], at_b(offset))
    await_bytes(part_b.at[pl.ds(0, nb - 1)], g_recv.at[1])
    part_c[ia] = jnp.sum(part_b[...], axis=0)
    for offset in off_a:
        send(part_c.at[ia], part_c.at[ia], 8, g_recv.at[2], at_a(offset)[1])
    await_bytes(part_c.at[pl.ds(0, na - 1)], g_recv.at[2])

    whole = part_c[...].reshape(dirs, dirs)
    upper, inverse = factor_and_inverse([whole[t : t + 8] for t in range(0, dirs, 8)])
    factor_ref[...] = upper
    inverse_high, inverse_low = split(inverse)
    inverse_twice = jnp.concatenate([inverse_high, inverse_high], axis=1)

    step_rows = 2
    turned_out = main.at[pl.ds(0, rows)]
    await_bytes(main.at[:, pl.ds(0, (nd - 1) * block), :], sends.at[5])

    def basis_step(j, carry):
        for t in range(step_rows):
            r = j * step_rows + t
            value = nn_dot(inverse_twice, both[r]) + nn_dot(inverse_low, both[r, 0:dirs, :])
            turned_out[r] = value.astype(BF16)
        for k in list(range(2, nd)) + [1]:
            q = lax.rem(d + k, nd)
            here = pl.ds(j * step_rows, step_rows)
            send(turned_out.at[here, dirs_at(q), :], out_ref.at[here, :, cols_at(d)], 9, o_recv.at[0], {"space": s, "dir": q})
        return carry

    lax.fori_loop(0, rows // step_rows, basis_step, 0)
    own_out = pltpu.make_async_copy(turned_out.at[:, dirs_at(d), :], out_ref.at[:, :, cols_at(d)], own_sem.at[1])
    own_out.start()
    await_bytes(halos.at[1, pl.ds(0, nd - 1)], sends.at[0])
    await_bytes(coef_in, sends.at[1])
    await_bytes(main.at[pl.ds(0, 2 * HALO), pl.ds(0, halves * block), :], sends.at[2])
    await_bytes(turned.at[:, :, pl.ds(0, (nd - 1) * quarter)], sends.at[3])
    await_bytes(halos.at[pl.ds(0, 2)], sends.at[4])
    await_bytes(part.at[pl.ds(0, na - 1)], sends.at[6])
    await_bytes(part_b.at[pl.ds(0, nb - 1)], sends.at[7])
    await_bytes(part_c.at[pl.ds(0, na - 1)], sends.at[8])
    own_out.wait()
    away = pl.ds(0, (nd - 1) * quarter)
    await_bytes(out_ref.at[:, :, away], o_recv.at[0])
    await_bytes(out_ref.at[:, :, away], sends.at[9])


def order_kernel(in_ref, factor_in, out_hbm, factor_out, ordered, out_sem, factor_sem):
    count = out_sem.shape[0]
    chunk = in_ref.shape[2] // count
    factor_copy = pltpu.make_async_copy(factor_in, factor_out, factor_sem.at[0])
    factor_copy.start()
    out = []
    for i in range(count):
        here = slice(i * chunk, (i + 1) * chunk)
        ordered[:, :, here] = jnp.swapaxes(in_ref[:, :, here].astype(F32), 0, 1).astype(BF16)
        there = pl.ds(i * chunk, chunk)
        out.append(pltpu.make_async_copy(ordered.at[:, :, there], out_hbm.at[:, :, there], out_sem.at[i]))
        out[i].start()
    for i in range(count):
        out[i].wait()
    factor_copy.wait()


def per_device(ns, nd, directions, depth_coef, sensitivity, obs_weight):
    group, rows, cols = directions.shape
    dirs = group * nd
    nx = 4 if ns >= 8 else ns // 2
    nz = ns // (2 * nx)
    na, nb = nx * nd, nz * 2
    tile = dirs // na
    quarter = cols // nd
    wide = quarter + 128
    ext = rows + 2 * HALO
    cfg = (nd, ns, nx, nz, rows, cols, dirs, rows * ns * cols)
    dma = pltpu.SemaphoreType.DMA
    turned, factor = pl.pallas_call(
        functools.partial(sketch_kernel, cfg),
        out_shape=(jax.ShapeDtypeStruct((rows, group, cols), BF16), jax.ShapeDtypeStruct((dirs, dirs), F32)),
        in_specs=[pl.BlockSpec(memory_space=pltpu.HBM)] * 4,
        out_specs=(pl.BlockSpec(memory_space=pltpu.VMEM),) * 2,
        scratch_shapes=[
            pltpu.VMEM((group, rows, cols), BF16),
            pltpu.VMEM((rows, cols), F32),
            pltpu.VMEM((rows, cols), F32),
            pltpu.VMEM((rows, cols), F32),
            pltpu.VMEM((rows, group, cols), BF16),
            pltpu.VMEM((nd, group, 128), BF16),
            pltpu.VMEM((ext, dirs, quarter), BF16),
            pltpu.VMEM((3, nd, group, 128), BF16),
            pltpu.VMEM((3, ext, wide), F32),
            pltpu.VMEM((3, rows, wide), F32),
            pltpu.VMEM((2, 3, rows, wide), F32),
            pltpu.VMEM((rows, 2 * dirs, quarter), BF16),
            pltpu.VMEM((2 * dirs, 2 * dirs), F32),
            pltpu.VMEM((na, tile, dirs), F32),
            pltpu.VMEM((nb, tile, dirs), F32),
            pltpu.VMEM((na, tile, dirs), F32),
            pltpu.VMEM((na, tile, dirs), F32),
            dma((10,)), dma((4,)), dma((4,)), dma((2,)), dma((1,)), dma((1,)), dma((3,)), dma((1,)), dma((3,)), dma((4,)),
        ],
        compiler_params=pltpu.CompilerParams(collective_id=0, has_side_effects=True, vmem_limit_bytes=40 * 2**20),
    )(*(pltpu.with_memory_space_constraint(x, pltpu.HBM) for x in (directions, depth_coef, sensitivity, obs_weight)))
    return pl.pallas_call(
        order_kernel,
        out_shape=(jax.ShapeDtypeStruct((group, rows, cols), BF16), jax.ShapeDtypeStruct((dirs, dirs), F32)),
        in_specs=[pl.BlockSpec(memory_space=pltpu.VMEM)] * 2,
        out_specs=(pl.BlockSpec(memory_space=pltpu.HBM),) * 2,
        scratch_shapes=[pltpu.VMEM((group, rows, cols), BF16), dma((4,)), dma((1,))],
        compiler_params=pltpu.CompilerParams(vmem_limit_bytes=40 * 2**20),
    )(turned, factor)


def solution(mesh):
    return jax.shard_map(
        functools.partial(per_device, mesh.shape["space"], mesh.shape["dir"]),
        mesh=mesh,
        in_specs=(P("dir", "space", None), P("space", None), P("space", None), P("space", None)),
        out_specs=(P("dir", "space", None), P()),
        check_vma=False,
    )
```

time: 80.8 us -> 67.3 us (0.83)
  Pallas kernels: 76.1 us -> 66.6 us
  local copies, waits for them, and re-layouts: 3.73 us -> 0 us
    pallas_call x1, Pallas kernels: 74.7 us -> 65.3 us  [per_device(): pl.pallas_call(functools.partial(sketch_kernel, cfg), out_shape=(jax.Shap...]
    unnamed x8 -> x0, local copies, waits for them, and re-layouts: 3.73 us -> none
where the time goes in v2:
time: 67.3 us; the launch traced here: 67.2 us
  Pallas kernels  66.6 us (99%)
    pallas_call x1, Pallas kernels, per_device(): pl.pallas_call(functools.partial(sketch_kernel, cfg), out_shape=(jax.Shap...  65.3 us

profile of v2, /device:TPU:1, one launch (start us, length us, event | category | flops | bytes accessed | tf_op | source)
XLA Modules:
  0.0 67.2 jit_solution(10325016348124210071)
XLA Ops:
  0.6 65.3 %shard_map.59 = (bf16[8,32,2048]{2,1,0:T(8,128)(2,1)S(1)}, f32[128,128]{1,0:T(8,128)S(1)}) custom-call(bf16[32,8,2048]{2,1,0:T(8,128)(2,1)} %dirs_hbm.1, f32[8,2048]{1,0:T(8,128)} %depth_hbm.1, f32[8,2048]{1,0:T(8,128)} %sens_hbm.1, f32[8,2048]{1,0:T(8,128)} %obs_hbm.1), custom_call_target="tpu_custom_call" | custom-call | tf_op jit(solution)/shard_map/pallas_call | solution.py:401
  66.0 1.2 %shard_map.60 = (bf16[32,8,2048]{2,1,0:T(8,128)(2,1)}, f32[128,128]{1,0:T(8,128)}) custom-call(bf16[8,32,2048]{2,1,0:T(8,128)(2,1)S(1)} %get-tuple-element.4.in_ref, f32[128,128]{1,0:T(8,128)S(1)} %get-tuple-element.5.factor_in), custom_call_target="tpu_custom_call" | custom-call | tf_op jit(solution)/shard_map/pallas_call | solution.py:428

commit v3 on v2

--- a/solution.py
+++ b/solution.py
@@ -83,7 +83,7 @@
 
 def sketch_kernel(
     cfg, dirs_hbm, depth_hbm, sens_hbm, obs_hbm, out_ref, factor_ref,
-    dirs_ref, depth_ref, sens_ref, obs_ref, turned, packs, main, halos, coef, coef_own, coef_in, both, gram, part, part_b, part_c, result,
+    dirs_ref, depth_ref, sens_ref, obs_ref, turned, packs, main, halos, coef, coef_own, coef_in, both, deal, gram, part, part_b, part_c, result,
     sends, y_recv, s_recv, pack_recv, own_recv, c_recv, g_recv, o_recv, own_sem, in_sem,
 ):
     nd, ns, nx, nz, rows, cols, dirs, total_cells = cfg
@@ -141,23 +141,29 @@
     lane = lax.broadcasted_iota(jnp.int32, (1, 128), 1)
     edge = (lane < HALO) | (lane >= 128 - HALO)
 
+    tiles = quarter // 128
+    line = lax.broadcasted_iota(jnp.int32, (quarter, quarter), 0)
+    spot = lax.broadcasted_iota(jnp.int32, (quarter, quarter), 1)
+    deal[...] = (lax.rem(spot, 128) * tiles + spot // 128 == line).astype(F32).astype(BF16)
+
     inputs[0].wait()
-    chunk = 256
-
-    def turn(j, carry):
-        here = pl.ds(pl.multiple_of(j * chunk, chunk), chunk)
-        turned[:, :, here] = jnp.swapaxes(dirs_ref[:, :, here].astype(F32), 0, 1).astype(BF16)
+
+    def turn(q, carry):
+        here = pl.ds(pl.multiple_of(q * quarter, quarter), quarter)
+        dealt = nn_dot(dirs_ref[:, :, here].astype(F32).reshape(group * rows, quarter).astype(BF16), deal[...])
+        turned[:, :, here] = jnp.swapaxes(dealt.reshape(group, rows, quarter), 0, 1).astype(BF16)
         return carry
 
-    lax.fori_loop(0, cols // chunk, turn, 0)
+    lax.fori_loop(0, nd, turn, 0)
 
     for q in range(nd):
+        def by_row(start, there):
+            return jnp.swapaxes(dirs_ref[:, :, start : start + 128].astype(F32), 0, 1) if there else jnp.zeros((rows, group, 128), F32)
+
+        beside = jnp.where(lane < 64, by_row((q + 1) * quarter, q < nd - 1), by_row(q * quarter - 128, q > 0))
         packed = jnp.zeros((group, 128), F32)
         for r in range(rows):
-            after = turned[r, :, (q + 1) * quarter : (q + 1) * quarter + 128].astype(F32) if q < nd - 1 else jnp.zeros((group, 128), F32)
-            before = turned[r, :, q * quarter - 128 : q * quarter].astype(F32) if q > 0 else jnp.zeros((group, 128), F32)
-            beside = jnp.where(lane < 64, after, before)
-            packed = jnp.where((lane >= 8 * r) & (lane < 8 * r + 8), pltpu.roll(beside, 8 * r + HALO, 1), packed)
+            packed = jnp.where((lane >= 8 * r) & (lane < 8 * r + 8), pltpu.roll(beside[r], 8 * r + HALO, 1), packed)
         packs[q] = packed.astype(BF16)
 
     for copy in inputs[1:]:
@@ -181,8 +187,6 @@
     above, below = {"space": up, "dir": d}, {"space": down, "dir": d}
     block = 16
     halves = group // block
-    parts = 2
-    part_cols = quarter // parts
 
     def dirs_at(g):
         return pl.ds(pl.multiple_of(g * group, group), group)
@@ -190,13 +194,18 @@
     def cols_at(q):
         return pl.ds(pl.multiple_of(q * quarter, 128), quarter)
 
-    def place(h, k, count=1):
-        return pl.ds((h * nd + k) * block, count * block)
+    blocks = [(0, h) for h in range(halves)] + [(k, h) for h in range(halves) for k in range(1, nd)]
+    stages = [[halves + h * (nd - 1) + k for k in range(nd - 1)] for h in range(halves)]
+    parts = 2
+    width = quarter // parts
+
+    def place(b, count=1):
+        return pl.ds(b * block, count * block)
 
     own_copies = [pltpu.make_async_copy(packs.at[d], halos.at[1, 0], own_sem.at[0])]
     for h in range(halves):
         own_copies.append(pltpu.make_async_copy(
-            turned.at[:, pl.ds(h * block, block), cols_at(d)], main.at[pl.ds(HALO, rows), place(h, 0), :], own_sem.at[1 + h]))
+            turned.at[:, pl.ds(h * block, block), cols_at(d)], main.at[pl.ds(HALO, rows), place(h), :], own_sem.at[1 + h]))
     for copy in own_copies:
         copy.start()
     for k in range(1, nd):
@@ -206,16 +215,17 @@
         send(coef_own, coef_in.at[side], 1, c_recv.at[0], peer)
     for h in range(halves):
         here = pl.ds(h * block, block)
-        send(turned.at[pl.ds(rows - HALO, HALO), here, cols_at(d)], main.at[pl.ds(0, HALO), place(h, 0), :], 2, own_recv.at[0], above)
-        send(turned.at[pl.ds(0, HALO), here, cols_at(d)], main.at[pl.ds(HALO + rows, HALO), place(h, 0), :], 2, own_recv.at[0], below)
-    for h in range(halves):
+        send(turned.at[pl.ds(rows - HALO, HALO), here, cols_at(d)], main.at[pl.ds(0, HALO), place(h), :], 2, own_recv.at[0], above)
+        send(turned.at[pl.ds(0, HALO), here, cols_at(d)], main.at[pl.ds(HALO + rows, HALO), place(h), :], 2, own_recv.at[0], below)
+    for n, stage in enumerate(stages):
         for p in range(parts):
-            for k in list(range(2, nd)) + [1]:
+            for b in stage[1:] + stage[:1]:
+                k, h = blocks[b]
                 q = lax.rem(d + k, nd)
-                there = pl.ds(pl.multiple_of(q * quarter + p * part_cols, 128), part_cols)
+                there = pl.ds(pl.multiple_of(q * quarter + p * width, 128), width)
                 send(turned.at[:, pl.ds(h * block, block), there],
-                     main.at[pl.ds(HALO, rows), place(h, k), pl.ds(p * part_cols, part_cols)],
-                     3, y_recv.at[h * parts + p], {"space": s, "dir": q})
+                     main.at[pl.ds(HALO, rows), place(b), pl.ds(p * width, width)],
+                     3, y_recv.at[n * parts + p], {"space": s, "dir": q})
     for copy in own_copies:
         copy.wait()
 
@@ -224,26 +234,40 @@
         coef[i, HALO : HALO + rows] = coef_own[i]
         coef[i, 0:HALO] = jnp.where(s > 0, coef_in[0, i, rows - HALO : rows], 0.0)
         coef[i, HALO + rows : ext] = jnp.where(s < ns - 1, coef_in[1, i, 0:HALO], 0.0)
+        plain = coef[i, :, 0:quarter]
+        high = plain.astype(BF16)
+        middle, low = split(plain - high.astype(F32))
+        dealt = nn_dot(jnp.concatenate([high, middle, low], axis=0), deal[...])
+        coef[i, :, 0:quarter] = (dealt[0:ext] + dealt[ext : 2 * ext]) + dealt[2 * ext : 3 * ext]
 
     await_bytes(halos.at[1, pl.ds(0, nd - 1)], pack_recv.at[0])
     for side, peer in enumerate((above, below)):
         send(halos.at[1], halos.at[2 * side], 4, pack_recv.at[1], peer)
 
-    def forward(h, p):
-        await_bytes(main.at[pl.ds(0, rows), pl.ds(0, (nd - 1) * block), pl.ds(0, part_cols)], y_recv.at[h * parts + p])
-        here = place(h, 1, nd - 1)
-        there = pl.ds(p * part_cols, part_cols)
-        send(main.at[pl.ds(rows, HALO), here, there], main.at[pl.ds(0, HALO), here, there], 5, s_recv.at[h * parts + p], above)
-        send(main.at[pl.ds(HALO, HALO), here, there], main.at[pl.ds(HALO + rows, HALO), here, there], 5, s_recv.at[h * parts + p], below)
-
-    def await_rows(h, p):
-        await_bytes(main.at[pl.ds(0, 2 * HALO), pl.ds(0, (nd - 1) * block), pl.ds(0, part_cols)], s_recv.at[h * parts + p])
-
-
-    def stencil(h, k):
-        held = pl.ds(pl.multiple_of((h * nd + k) * block, block), block)
+    def forward(n, p):
+        here, there = place(stages[n][0], len(stages[n])), pl.ds(p * width, width)
+        number = n * parts + p
+        await_bytes(main.at[pl.ds(0, rows), here, there], y_recv.at[number])
+        send(main.at[pl.ds(rows, HALO), here, there], main.at[pl.ds(0, HALO), here, there], 5, s_recv.at[number], above)
+        send(main.at[pl.ds(HALO, HALO), here, there], main.at[pl.ds(HALO + rows, HALO), here, there], 5, s_recv.at[number], below)
+
+    def await_rows(n, p):
+        here, there = place(stages[n][0], len(stages[n])), pl.ds(p * width, width)
+        await_bytes(main.at[pl.ds(0, 2 * HALO), here, there], s_recv.at[n * parts + p])
+
+    def stencil(b):
+        held = pl.ds(pl.multiple_of(b * block, block), block)
+        late = jnp.maximum(b - halves, 0)
+        k = jnp.where(b < halves, 0, 1 + lax.rem(late, nd - 1))
+        h = jnp.where(b < halves, b, late // (nd - 1))
+        of_owner = pl.ds(pl.multiple_of(h * block, block), block)
         base = lax.rem(d + nd - k, nd) * group + h * block
         here = pl.ds(pl.multiple_of(base, block), block)
+
+        first, last = lane == 0, lane == 127
+
+        def cut(row):
+            return [row[:, 128 * t : 128 * t + 128] for t in range(tiles)]
 
         def raw(e):
             if e < HALO:
@@ -252,67 +276,79 @@
                 side, r = 1, e - HALO
             else:
                 side, r = 2, e - HALO - rows
-            beside = pltpu.roll(halos[side, k, h * block : (h + 1) * block, :].astype(F32), (128 - 8 * r - HALO) % 128, 1)
-            row = jnp.concatenate([main[e, held, :].astype(F32), jnp.where(edge, beside, 0.0)], axis=1)
+            beside = pltpu.roll(halos[side, k, of_owner, :].astype(F32), (128 - 8 * r - HALO) % 128, 1)
+            row = cut(main[e, held, :].astype(F32)) + [jnp.where(edge, beside, 0.0)]
             if side == 0:
-                row = jnp.where(s > 0, row, 0.0)
+                row = [jnp.where(s > 0, v, 0.0) for v in row]
             if side == 2:
-                row = jnp.where(s < ns - 1, row, 0.0)
+                row = [jnp.where(s < ns - 1, v, 0.0) for v in row]
             return row
 
-        def around(above, row, below):
-            return (above + below) + (pltpu.roll(row, 1, 1) + pltpu.roll(row, wide - 1, 1))
-
+        def beside_of(row):
+            next_first, next_out = pltpu.roll(row[0], 127, 1), pltpu.roll(row[tiles], 127, 1)
+            last_last, last_out = pltpu.roll(row[tiles - 1], 1, 1), pltpu.roll(row[tiles], 1, 1)
+            right = row[1:tiles] + [jnp.where(last, next_out, next_first), jnp.where(last, next_first, next_out)]
+            left = [jnp.where(first, last_out, last_last)] + row[0 : tiles - 1] + [jnp.where(first, last_last, last_out)]
+            return [a + b for a, b in zip(left, right)]
+
+        def of_row(n, j):
+            row = coef[n, j : j + 1]
+            return cut(row) + [row[:, quarter:wide]]
+
+        def around(rows_of, j, own):
+            return [
+                (a + b) + (n + w * v)
+                for a, b, n, w, v in zip(rows_of[j - 1], rows_of[j + 1], beside_of(rows_of[j]), own, rows_of[j])]
+
+        def times(a, b):
+            return [v * w for v, w in zip(a, b)]
+
+        six = [6.0] * (tiles + 1)
         field, state, flux, source = {}, {}, {}, {}
         for e in range(ext):
             field[e] = raw(e)
             j = e - 1
             if j >= 1:
-                state[j] = coef[0, j : j + 1] * (around(field[j - 1], field[j], field[j + 1]) + 6.0 * field[j])
+                state[j] = times(of_row(0, j), around(field, j, six))
             j = e - 2
             if j >= 2:
-                flux[j] = coef[2, j : j + 1] * (around(state[j - 1], state[j], state[j + 1]) + coef[1, j : j + 1] * state[j])
+                flux[j] = times(of_row(2, j), around(state, j, of_row(1, j)))
             j = e - 3
             if j >= 3:
-                source[j] = coef[0, j : j + 1] * (around(flux[j - 1], flux[j], flux[j + 1]) + coef[1, j : j + 1] * flux[j])
+                source[j] = times(of_row(0, j), around(flux, j, of_row(1, j)))
             j = e - 4
             if j >= 4:
-                value = field[j] + 0.1 * (around(source[j - 1], source[j], source[j + 1]) + 6.0 * source[j])
-                high, low = split(value[:, :quarter])
+                value = [v + 0.1 * w for v, w in zip(field[j], around(source, j, six))]
+                high, low = split(jnp.concatenate(value[:tiles], axis=1))
                 both[j - HALO, here, :] = high
                 both[j - HALO, pl.ds(pl.multiple_of(dirs + base, block), block), :] = low
 
-    def stencils(h, first, last):
-        def step(k, carry):
-            stencil(h, k)
-            return carry
-
-        lax.fori_loop(first, last, step, 0)
-
-    stages = [(h, p) for h in range(halves) for p in range(parts)]
-    forward(*stages[0])
     await_bytes(main.at[pl.ds(0, 2 * HALO), pl.ds(0, halves * block), :], own_recv.at[0])
     await_bytes(halos.at[pl.ds(0, 2)], pack_recv.at[1])
-    stencils(0, 0, 1)
-    forward(*stages[1])
-    stencils(1, 0, 1)
-    forward(*stages[2])
-    for p in range(parts):
-        await_rows(0, p)
-    stencils(0, 1, 2)
-    forward(*stages[3])
-    stencils(0, 2, nd)
-    for p in range(parts):
-        await_rows(1, p)
-    stencils(1, 1, nd)
-
-    gram[...] = jnp.zeros_like(gram)
-
-    def gram_step(r, carry):
-        gram[...] += nt_dot(both[r], both[r])
+    before = {b: [] for b in range(len(blocks))}
+    for n, stage in enumerate(stages):
+        for p in range(parts):
+            before[n * parts + p].append(functools.partial(forward, n, p))
+    for n, stage in enumerate(stages):
+        for p in range(parts):
+            before[stage[0]].append(functools.partial(await_rows, n, p))
+
+    def step(b, carry):
+        for at, actions in before.items():
+            if actions:
+                @pl.when(b == at)
+                def _():
+                    for action in actions:
+                        action()
+        stencil(b)
         return carry
 
-    lax.fori_loop(0, rows, gram_step, 0)
+    lax.fori_loop(0, len(blocks), step, 0)
+
+    total = nt_dot(both[0], both[0])
+    for r in range(1, rows):
+        total = total + nt_dot(both[r], both[r])
+    gram[...] = total
     mixed = gram[0:dirs, dirs : 2 * dirs] + gram[dirs : 2 * dirs, 0:dirs]
     local = (gram[0:dirs, 0:dirs] + gram[dirs : 2 * dirs, dirs : 2 * dirs] + mixed) * (1.0 / total_cells)
     result[...] = local.reshape(na, tile, dirs)
@@ -321,6 +357,14 @@
         i, peer = at_a(offset)
         send(result.at[i], part.at[ia], 6, g_recv.at[0], peer)
     part[ia] = result[ia]
+
+    deal[...] = (lax.rem(line, 128) * tiles + line // 128 == spot).astype(F32).astype(BF16)
+
+    def undeal(r, carry):
+        both[r] = nn_dot(both[r], deal[...]).astype(BF16)
+        return carry
+
+    lax.fori_loop(0, rows, undeal, 0)
     await_bytes(part.at[pl.ds(0, na - 1)], g_recv.at[0])
     part_b[ib] = jnp.sum(part[...], axis=0)
     for offset in off_b:
@@ -416,6 +460,7 @@
             pltpu.VMEM((3, rows, wide), F32),
             pltpu.VMEM((2, 3, rows, wide), F32),
             pltpu.VMEM((rows, 2 * dirs, quarter), BF16),
+            pltpu.VMEM((quarter, quarter), BF16),
             pltpu.VMEM((2 * dirs, 2 * dirs), F32),
             pltpu.VMEM((na, tile, dirs), F32),
             pltpu.VMEM((nb, tile, dirs), F32),

time: 67.3 us -> 65.2 us (0.969)
  Pallas kernels: 66.6 us -> 64.5 us
    pallas_call x1, Pallas kernels: 65.3 us -> 63.3 us  [per_device(): pl.pallas_call(functools.partial(sketch_kernel, cfg), out_shape=(jax.Shap...]
where the time goes in v3:
time: 65.2 us; the launch traced here: 65.1 us
  Pallas kernels  64.5 us (99%)
    pallas_call x1, Pallas kernels, per_device(): pl.pallas_call(functools.partial(sketch_kernel, cfg), out_shape=(jax.Shap...  63.3 us

profile of v3, /device:TPU:1, one launch (start us, length us, event | category | flops | bytes accessed | tf_op | source)
XLA Modules:
  0.0 65.1 jit_solution(11663244868121184777)
XLA Ops:
  0.6 63.3 %shard_map.59 = (bf16[8,32,2048]{2,1,0:T(8,128)(2,1)S(1)}, f32[128,128]{1,0:T(8,128)S(1)}) custom-call(bf16[32,8,2048]{2,1,0:T(8,128)(2,1)} %dirs_hbm.1, f32[8,2048]{1,0:T(8,128)} %depth_hbm.1, f32[8,2048]{1,0:T(8,128)} %sens_hbm.1, f32[8,2048]{1,0:T(8,128)} %obs_hbm.1), custom_call_target="tpu_custom_call" | custom-call | tf_op jit(solution)/shard_map/pallas_call | solution.py:445
  63.9 1.2 %shard_map.60 = (bf16[32,8,2048]{2,1,0:T(8,128)(2,1)}, f32[128,128]{1,0:T(8,128)}) custom-call(bf16[8,32,2048]{2,1,0:T(8,128)(2,1)S(1)} %get-tuple-element.4.in_ref, f32[128,128]{1,0:T(8,128)S(1)} %get-tuple-element.5.factor_in), custom_call_target="tpu_custom_call" | custom-call | tf_op jit(solution)/shard_map/pallas_call | solution.py:473

commit v4 on v3

--- a/solution.py
+++ b/solution.py
@@ -194,8 +194,11 @@
     def cols_at(q):
         return pl.ds(pl.multiple_of(q * quarter, 128), quarter)
 
-    blocks = [(0, h) for h in range(halves)] + [(k, h) for h in range(halves) for k in range(1, nd)]
-    stages = [[halves + h * (nd - 1) + k for k in range(nd - 1)] for h in range(halves)]
+    owners = [1, nd - 1] + list(range(2, nd - 1))
+    blocks = [(0, h) for h in range(halves)] + [(k, h) for h in range(halves) for k in owners]
+    final = len(blocks) - len(owners)
+    stages = [list(range(b, b + len(owners))) for b in range(halves, final, len(owners))] + [[b] for b in range(final, len(blocks))]
+    whole_stages = len(stages) - len(owners)
     parts = 2
     width = quarter // parts
 
@@ -217,9 +220,11 @@
         here = pl.ds(h * block, block)
         send(turned.at[pl.ds(rows - HALO, HALO), here, cols_at(d)], main.at[pl.ds(0, HALO), place(h), :], 2, own_recv.at[0], above)
         send(turned.at[pl.ds(0, HALO), here, cols_at(d)], main.at[pl.ds(HALO + rows, HALO), place(h), :], 2, own_recv.at[0], below)
-    for n, stage in enumerate(stages):
+    rounds = [[n] for n in range(whole_stages)] + [list(range(whole_stages, len(stages)))]
+    for round_stages in rounds:
         for p in range(parts):
-            for b in stage[1:] + stage[:1]:
+            pieces = [(n, b) for n in round_stages for b in stages[n]]
+            for n, b in pieces[2:] + pieces[:2]:
                 k, h = blocks[b]
                 q = lax.rem(d + k, nd)
                 there = pl.ds(pl.multiple_of(q * quarter + p * width, 128), width)
@@ -258,7 +263,8 @@
     def stencil(b):
         held = pl.ds(pl.multiple_of(b * block, block), block)
         late = jnp.maximum(b - halves, 0)
-        k = jnp.where(b < halves, 0, 1 + lax.rem(late, nd - 1))
+        turn_of = lax.rem(late, nd - 1)
+        k = jnp.where(b < halves, 0, jnp.where(turn_of == 0, 1, jnp.where(turn_of == 1, nd - 1, turn_of)))
         h = jnp.where(b < halves, b, late // (nd - 1))
         of_owner = pl.ds(pl.multiple_of(h * block, block), block)
         base = lax.rem(d + nd - k, nd) * group + h * block
@@ -326,9 +332,10 @@
     await_bytes(main.at[pl.ds(0, 2 * HALO), pl.ds(0, halves * block), :], own_recv.at[0])
     await_bytes(halos.at[pl.ds(0, 2)], pack_recv.at[1])
     before = {b: [] for b in range(len(blocks))}
-    for n, stage in enumerate(stages):
+    for i, round_stages in enumerate(rounds):
         for p in range(parts):
-            before[n * parts + p].append(functools.partial(forward, n, p))
+            for n in round_stages:
+                before[i * parts + p].append(functools.partial(forward, n, p))
     for n, stage in enumerate(stages):
         for p in range(parts):
             before[stage[0]].append(functools.partial(await_rows, n, p))
@@ -466,7 +473,7 @@
             pltpu.VMEM((nb, tile, dirs), F32),
             pltpu.VMEM((na, tile, dirs), F32),
             pltpu.VMEM((na, tile, dirs), F32),
-            dma((10,)), dma((4,)), dma((4,)), dma((2,)), dma((1,)), dma((1,)), dma((3,)), dma((1,)), dma((3,)), dma((4,)),
+            dma((10,)), dma((8,)), dma((8,)), dma((2,)), dma((1,)), dma((1,)), dma((3,)), dma((1,)), dma((3,)), dma((4,)),
         ],
         compiler_params=pltpu.CompilerParams(collective_id=0, has_side_effects=True, vmem_limit_bytes=40 * 2**20),
     )(*(pltpu.with_memory_space_constraint(x, pltpu.HBM) for x in (directions, depth_coef, sensitivity, obs_weight)))

time: 65.2 us -> 64.5 us (0.989)
  Pallas kernels: 64.5 us -> 63.8 us
    pallas_call x1, Pallas kernels: 63.3 us -> 62.5 us  [per_device(): pl.pallas_call(functools.partial(sketch_kernel, cfg), out_shape=(jax.Shap...]
where the time goes in v4:
time: 64.5 us; the launch traced here: 64.4 us
  Pallas kernels  63.8 us (99%)
    pallas_call x1, Pallas kernels, per_device(): pl.pallas_call(functools.partial(sketch_kernel, cfg), out_shape=(jax.Shap...  62.5 us

profile of v4, /device:TPU:1, one launch (start us, length us, event | category | flops | bytes accessed | tf_op | source)
XLA Modules:
  0.0 64.4 jit_solution(1547853514980290620)
XLA Ops:
  0.6 62.5 %shard_map.59 = (bf16[8,32,2048]{2,1,0:T(8,128)(2,1)S(1)}, f32[128,128]{1,0:T(8,128)S(1)}) custom-call(bf16[32,8,2048]{2,1,0:T(8,128)(2,1)} %dirs_hbm.1, f32[8,2048]{1,0:T(8,128)} %depth_hbm.1, f32[8,2048]{1,0:T(8,128)} %sens_hbm.1, f32[8,2048]{1,0:T(8,128)} %obs_hbm.1), custom_call_target="tpu_custom_call" | custom-call | tf_op jit(solution)/shard_map/pallas_call | solution.py:452
  63.2 1.2 %shard_map.60 = (bf16[32,8,2048]{2,1,0:T(8,128)(2,1)}, f32[128,128]{1,0:T(8,128)}) custom-call(bf16[8,32,2048]{2,1,0:T(8,128)(2,1)S(1)} %get-tuple-element.4.in_ref, f32[128,128]{1,0:T(8,128)S(1)} %get-tuple-element.5.factor_in), custom_call_target="tpu_custom_call" | custom-call | tf_op jit(solution)/shard_map/pallas_call | solution.py:480

commit v5 on v4

--- a/solution.py
+++ b/solution.py
@@ -47,35 +47,37 @@
         x, o = tiles[p], 8 * p
         columns = [spread(x[:, o + j : o + j + 1]) for j in range(8)]
         e = {(i, j): spread(columns[j][i : i + 1]) for j in range(8) for i in range(j, 8)}
-        r, l, w, q = [], {}, {}, {}
+        r, l, f, unit, w = [], {}, {}, {}, {}
         for j in range(8):
+            over = 1.0 / e[j, j]
             r.append(lax.rsqrt(e[j, j]))
             for i in range(j + 1, 8):
+                f[i, j] = e[i, j] * over
                 l[i, j] = e[i, j] * r[j]
             for i in range(j + 1, 8):
                 for k in range(j + 1, i + 1):
-                    e[i, k] = e[i, k] - l[i, j] * l[k, j]
+                    e[i, k] = e[i, k] - (e[i, j] * e[k, j]) * over
+        for j in range(8):
+            for i in range(j + 1, 8):
+                unit[i, j] = -tree_sum([f[i, j]] + [f[i, k] * unit[k, j] for k in range(j + 1, i)])
         for j in range(8):
             w[j, j] = r[j]
             for i in range(j + 1, 8):
-                w[i, j] = -r[i] * tree_sum([l[i, k] * w[k, j] for k in range(j, i)])
-        for i in range(8):
-            for j in range(i, 8):
-                q[i, j] = q[j, i] = tree_sum([w[k, i] * w[k, j] for k in range(j, 8)])
+                w[i, j] = r[i] * unit[i, j]
         panel = (lane >= o) & (lane < o + 8)
         rows = [spread(v) for v in jnp.split(jnp.where(panel, jnp.where(lane - o == sub, 1.0, 0.0), x), 8, axis=0)]
-        scaled = [tree_sum([q[i, j] * rows[j] for j in range(8)]) for i in range(8)]
+        solved = [tree_sum([w[j, i] * rows[i] for i in range(j + 1)]) for j in range(8)]
+        scaled = [tree_sum([w[j, i] * solved[j] for j in range(i, 8)]) for i in range(8)]
         for t in range(p + 1, len(tiles)):
             taken = tree_sum([spread(tiles[t][:, o + j : o + j + 1]) * scaled[j] for j in range(8)])
             tiles[t] = jnp.where(panel, 0.0, tiles[t]) - taken
-        weights = []
+        below = solved[0]
+        for j in range(1, 8):
+            below = jnp.where(sub == j, solved[j], below)
+        above = below
         for j in range(8):
-            column = jnp.where(sub == j, w[j, j], 0.0)
-            for i in range(j + 1, 8):
-                column = jnp.where(sub == i, w[i, j], column)
-            weights.append(column)
-        below = tree_sum([weights[j] * rows[j] for j in range(8)])
-        above = tree_sum([weights[j] * spread(x[j : j + 1]) for j in range(8)])
+            for i in range(j, 8):
+                above = jnp.where((sub == j) & (lane == o + i), e[j, j] * r[j] if i == j else l[i, j], above)
         inverse.append(jnp.where(lane < o + 8, below, 0.0))
         upper.append(jnp.where(lane >= o + sub, above, 0.0))
     return jnp.concatenate(upper, axis=0), jnp.concatenate(inverse, axis=0)
@@ -83,7 +85,7 @@
 
 def sketch_kernel(
     cfg, dirs_hbm, depth_hbm, sens_hbm, obs_hbm, out_ref, factor_ref,
-    dirs_ref, depth_ref, sens_ref, obs_ref, turned, packs, main, halos, coef, coef_own, coef_in, both, deal, gram, part, part_b, part_c, result,
+    dirs_ref, depth_ref, sens_ref, obs_ref, turned, packs, main, halos, coef, coef_own, coef_in, both, values, deal, gram, part, part_b, part_c, result,
     sends, y_recv, s_recv, pack_recv, own_recv, c_recv, g_recv, o_recv, own_sem, in_sem,
 ):
     nd, ns, nx, nz, rows, cols, dirs, total_cells = cfg
@@ -275,15 +277,15 @@
         def cut(row):
             return [row[:, 128 * t : 128 * t + 128] for t in range(tiles)]
 
-        def raw(e):
+        def raw(e, part):
             if e < HALO:
                 side, r = 0, rows - HALO + e
             elif e < HALO + rows:
                 side, r = 1, e - HALO
             else:
                 side, r = 2, e - HALO - rows
-            beside = pltpu.roll(halos[side, k, of_owner, :].astype(F32), (128 - 8 * r - HALO) % 128, 1)
-            row = cut(main[e, held, :].astype(F32)) + [jnp.where(edge, beside, 0.0)]
+            beside = pltpu.roll(halos[side, k, of_owner, :].astype(F32)[part], (128 - 8 * r - HALO) % 128, 1)
+            row = cut(main[e, held, :].astype(F32)[part]) + [jnp.where(edge, beside, 0.0)]
             if side == 0:
                 row = [jnp.where(s > 0, v, 0.0) for v in row]
             if side == 2:
@@ -310,32 +312,41 @@
             return [v * w for v, w in zip(a, b)]
 
         six = [6.0] * (tiles + 1)
-        field, state, flux, source = {}, {}, {}, {}
-        for e in range(ext):
-            field[e] = raw(e)
-            j = e - 1
-            if j >= 1:
-                state[j] = times(of_row(0, j), around(field, j, six))
-            j = e - 2
-            if j >= 2:
-                flux[j] = times(of_row(2, j), around(state, j, of_row(1, j)))
-            j = e - 3
-            if j >= 3:
-                source[j] = times(of_row(0, j), around(flux, j, of_row(1, j)))
-            j = e - 4
-            if j >= 4:
-                value = [v + 0.1 * w for v, w in zip(field[j], around(source, j, six))]
-                high, low = split(jnp.concatenate(value[:tiles], axis=1))
-                both[j - HALO, here, :] = high
-                both[j - HALO, pl.ds(pl.multiple_of(dirs + base, block), block), :] = low
-
-    await_bytes(main.at[pl.ds(0, 2 * HALO), pl.ds(0, halves * block), :], own_recv.at[0])
-    await_bytes(halos.at[pl.ds(0, 2)], pack_recv.at[1])
+        for start in range(0, block, 8):
+            part = slice(start, start + 8)
+            field, state, flux, source = {}, {}, {}, {}
+            for e in range(ext):
+                field[e] = raw(e, part)
+                j = e - 1
+                if j >= 1:
+                    state[j] = times(of_row(0, j), around(field, j, six))
+                j = e - 2
+                if j >= 2:
+                    flux[j] = times(of_row(2, j), around(state, j, of_row(1, j)))
+                j = e - 3
+                if j >= 3:
+                    source[j] = times(of_row(0, j), around(flux, j, of_row(1, j)))
+                j = e - 4
+                if j >= 4:
+                    again = cut(main[j, held, :].astype(F32)[part])
+                    value = [v + 0.1 * w for v, w in zip(again, around(source, j, six))]
+                    values[j - HALO, part, :] = jnp.concatenate(value, axis=1)
+        for r in range(rows):
+            high, low = split(values[r])
+            both[r, here, :] = high
+            both[r, pl.ds(pl.multiple_of(dirs + base, block), block), :] = low
+
     before = {b: [] for b in range(len(blocks))}
+
+    def await_own():
+        await_bytes(main.at[pl.ds(0, 2 * HALO), pl.ds(0, halves * block), :], own_recv.at[0])
+        await_bytes(halos.at[pl.ds(0, 2)], pack_recv.at[1])
+
     for i, round_stages in enumerate(rounds):
         for p in range(parts):
             for n in round_stages:
                 before[i * parts + p].append(functools.partial(forward, n, p))
+    before[0].append(await_own)
     for n, stage in enumerate(stages):
         for p in range(parts):
             before[stage[0]].append(functools.partial(await_rows, n, p))
@@ -467,6 +478,7 @@
             pltpu.VMEM((3, rows, wide), F32),
             pltpu.VMEM((2, 3, rows, wide), F32),
             pltpu.VMEM((rows, 2 * dirs, quarter), BF16),
+            pltpu.VMEM((rows, 16, quarter), F32),
             pltpu.VMEM((quarter, quarter), BF16),
             pltpu.VMEM((2 * dirs, 2 * dirs), F32),
             pltpu.VMEM((na, tile, dirs), F32),

time: 64.5 us -> 63.9 us (level)
  no operation moved by 1% of the time
where the time goes in v5:
time: 63.9 us; the launch traced here: 63.8 us
  Pallas kernels  63.2 us (99%)
  between operations  0.64 us (1%)
    pallas_call x1, Pallas kernels, per_device(): pl.pallas_call(functools.partial(sketch_kernel, cfg), out_shape=(jax.Shap...  62 us

profile of v5, /device:TPU:1, one launch (start us, length us, event | category | flops | bytes accessed | tf_op | source)
XLA Modules:
  0.0 63.8 jit_solution(6492769362331060187)
XLA Ops:
  0.6 62.0 %shard_map.59 = (bf16[8,32,2048]{2,1,0:T(8,128)(2,1)S(1)}, f32[128,128]{1,0:T(8,128)S(1)}) custom-call(bf16[32,8,2048]{2,1,0:T(8,128)(2,1)} %dirs_hbm.1, f32[8,2048]{1,0:T(8,128)} %depth_hbm.1, f32[8,2048]{1,0:T(8,128)} %sens_hbm.1, f32[8,2048]{1,0:T(8,128)} %obs_hbm.1), custom_call_target="tpu_custom_call" | custom-call | tf_op jit(solution)/shard_map/pallas_call | solution.py:463
  62.6 1.2 %shard_map.60 = (bf16[32,8,2048]{2,1,0:T(8,128)(2,1)}, f32[128,128]{1,0:T(8,128)}) custom-call(bf16[8,32,2048]{2,1,0:T(8,128)(2,1)S(1)} %get-tuple-element.4.in_ref, f32[128,128]{1,0:T(8,128)S(1)} %get-tuple-element.5.factor_in), custom_call_target="tpu_custom_call" | custom-call | tf_op jit(solution)/shard_map/pallas_call | solution.py:492

commit v6 on v5

--- a/solution.py
+++ b/solution.py
@@ -201,7 +201,7 @@
     final = len(blocks) - len(owners)
     stages = [list(range(b, b + len(owners))) for b in range(halves, final, len(owners))] + [[b] for b in range(final, len(blocks))]
     whole_stages = len(stages) - len(owners)
-    parts = 2
+    parts = 1
     width = quarter // parts
 
     def place(b, count=1):

time: 63.9 us -> 62.7 us (0.981)
  Pallas kernels: 63.2 us -> 62 us
    pallas_call x1, Pallas kernels: 62 us -> 60.8 us  [per_device(): pl.pallas_call(functools.partial(sketch_kernel, cfg), out_shape=(jax.Shap...]
where the time goes in v6:
time: 62.7 us; the launch traced here: 62.6 us
  Pallas kernels  62 us (99%)
  between operations  0.64 us (1%)
    pallas_call x1, Pallas kernels, per_device(): pl.pallas_call(functools.partial(sketch_kernel, cfg), out_shape=(jax.Shap...  60.8 us

profile of v6, /device:TPU:1, one launch (start us, length us, event | category | flops | bytes accessed | tf_op | source)
XLA Modules:
  0.0 62.6 jit_solution(7153569634751247742)
XLA Ops:
  0.6 60.8 %shard_map.59 = (bf16[8,32,2048]{2,1,0:T(8,128)(2,1)S(1)}, f32[128,128]{1,0:T(8,128)S(1)}) custom-call(bf16[32,8,2048]{2,1,0:T(8,128)(2,1)} %dirs_hbm.1, f32[8,2048]{1,0:T(8,128)} %depth_hbm.1, f32[8,2048]{1,0:T(8,128)} %sens_hbm.1, f32[8,2048]{1,0:T(8,128)} %obs_hbm.1), custom_call_target="tpu_custom_call" | custom-call | tf_op jit(solution)/shard_map/pallas_call | solution.py:463
  61.4 1.2 %shard_map.60 = (bf16[32,8,2048]{2,1,0:T(8,128)(2,1)}, f32[128,128]{1,0:T(8,128)}) custom-call(bf16[8,32,2048]{2,1,0:T(8,128)(2,1)S(1)} %get-tuple-element.4.in_ref, f32[128,128]{1,0:T(8,128)S(1)} %get-tuple-element.5.factor_in), custom_call_target="tpu_custom_call" | custom-call | tf_op jit(solution)/shard_map/pallas_call | solution.py:492

commit v7 on v6

--- a/solution.py
+++ b/solution.py
@@ -198,9 +198,7 @@
 
     owners = [1, nd - 1] + list(range(2, nd - 1))
     blocks = [(0, h) for h in range(halves)] + [(k, h) for h in range(halves) for k in owners]
-    final = len(blocks) - len(owners)
-    stages = [list(range(b, b + len(owners))) for b in range(halves, final, len(owners))] + [[b] for b in range(final, len(blocks))]
-    whole_stages = len(stages) - len(owners)
+    stages = [[b] for b in range(halves, len(blocks))]
     parts = 1
     width = quarter // parts
 
@@ -222,7 +220,7 @@
         here = pl.ds(h * block, block)
         send(turned.at[pl.ds(rows - HALO, HALO), here, cols_at(d)], main.at[pl.ds(0, HALO), place(h), :], 2, own_recv.at[0], above)
         send(turned.at[pl.ds(0, HALO), here, cols_at(d)], main.at[pl.ds(HALO + rows, HALO), place(h), :], 2, own_recv.at[0], below)
-    rounds = [[n] for n in range(whole_stages)] + [list(range(whole_stages, len(stages)))]
+    rounds = [list(range(n, n + len(owners))) for n in range(0, len(stages), len(owners))]
     for round_stages in rounds:
         for p in range(parts):
             pieces = [(n, b) for n in round_stages for b in stages[n]]

time: 62.7 us -> 62.8 us (level)
  no operation moved by 1% of the time
where the time goes in v7:
time: 62.8 us; the launch traced here: 62.7 us
  Pallas kernels  62 us (99%)
  between operations  0.64 us (1%)
    pallas_call x1, Pallas kernels, per_device(): pl.pallas_call(functools.partial(sketch_kernel, cfg), out_shape=(jax.Shap...  60.8 us

profile of v7, /device:TPU:1, one launch (start us, length us, event | category | flops | bytes accessed | tf_op | source)
XLA Modules:
  0.0 62.7 jit_solution(1061106803142534190)
XLA Ops:
  0.6 60.8 %shard_map.59 = (bf16[8,32,2048]{2,1,0:T(8,128)(2,1)S(1)}, f32[128,128]{1,0:T(8,128)S(1)}) custom-call(bf16[32,8,2048]{2,1,0:T(8,128)(2,1)} %dirs_hbm.1, f32[8,2048]{1,0:T(8,128)} %depth_hbm.1, f32[8,2048]{1,0:T(8,128)} %sens_hbm.1, f32[8,2048]{1,0:T(8,128)} %obs_hbm.1), custom_call_target="tpu_custom_call" | custom-call | tf_op jit(solution)/shard_map/pallas_call | solution.py:461
  61.4 1.2 %shard_map.60 = (bf16[32,8,2048]{2,1,0:T(8,128)(2,1)}, f32[128,128]{1,0:T(8,128)}) custom-call(bf16[8,32,2048]{2,1,0:T(8,128)(2,1)S(1)} %get-tuple-element.4.in_ref, f32[128,128]{1,0:T(8,128)S(1)} %get-tuple-element.5.factor_in), custom_call_target="tpu_custom_call" | custom-call | tf_op jit(solution)/shard_map/pallas_call | solution.py:490
